TPU v7x, 256 devices: a whole 4x4x8 slice. The times are simulated.
256 devices in a mesh: gx: 8 (over y, core), gy: 32 (over x, z).
Axes of the slice: x: 4, y: 4, z: 8, core: 2. Of those that a mesh axis runs over, the one named last changes fastest.
Arguments:
- free_velocity: float32 [8, 32, 6, 2048], P('gx', 'gy'), may hold values from -6 to 6
- body_radius: float32 [8, 32, 2048], P('gx', 'gy'), may hold values from 0.8 to 1.25
- face_lists: int32 [8, 32, 4, 256], P('gx', 'gy'), may hold values from 0 to 2047
- corner_lists: int32 [8, 32, 4, 32], P('gx', 'gy'), may hold values from 0 to 2047
- owner_body: int32 [8, 32, 4096], P('gx', 'gy'), may hold values from 0 to 2047
- other_body: int32 [8, 32, 4096], P('gx', 'gy'), may hold values from 0 to 3199
- contact_angles: float32 [8, 32, 2, 4096], P('gx', 'gy'), may hold values from -3.140625 to 3.140625
- contact_arms: float32 [8, 32, 2, 4096], P('gx', 'gy'), may hold values from 0.8 to 1.25
- friction: float32 [8, 32, 4096], P('gx', 'gy'), may hold values from 0.2 to 0.6
- approach: float32 [8, 32, 4096], P('gx', 'gy'), may hold values from -3 to 3
- start_impulse: float32 [8, 32, 3, 4096], P('gx', 'gy'), may hold values from -3 to 3
Outputs:
- velocity: float32 [8, 32, 6, 2048], P('gx', 'gy')
- impulse: float32 [8, 32, 3, 4096], P('gx', 'gy')
Inputs may be any that keep to these rules, and one draw needn't show every extreme that they name: `other_body`: columns below 2048 of the extended table are owned spheres; the rest are the copy blocks in the order of the statement. `face_lists`: indices of owned spheres; a sphere may stand in several lists. `corner_lists`: indices of owned spheres. `owner_body`: indices of owned spheres.
All inputs are finite; a program needn't handle non-finite values.
Results may differ from a plain program's by a relative error of at most 0.0003.
Values sent between devices are 32-bit elements; how exact they have to be, the bound alone decides.
No kernel may reach another device: no remote copies, remote signals or barrier semaphores. Data moves between devices by JAX's collectives and lax.ppermute only.
A program may use at most 64 MiB of HBM per device.

v0:
```python
import jax
import jax.numpy as jnp
from jax import lax
from jax.sharding import PartitionSpec as P

SWEEPS = 4


RELAX = 0.25
SMALLEST = 1e-20


def padded_2(shard, sides, width):
    for axis, dim in sides:
        size, length = (lax.axis_size(axis), shard.shape[dim])
        up = [(i, (i + 1) % size) for i in range(size - 1)]
        down = [(j, i) for i, j in up]
        last = lax.slice_in_dim(shard, length - width, length, axis=dim)
        first = lax.slice_in_dim(shard, 0, width, axis=dim)
        before = lax.ppermute(last, axis, up)
        after = lax.ppermute(first, axis, down)
        shard = jnp.concatenate([before, shard, after], axis=dim)
    return shard


def frames(angles):
    cos_polar = jnp.cos(angles[0])
    sin_polar = jnp.sin(angles[0])
    cos_azim = jnp.cos(angles[1])
    sin_azim = jnp.sin(angles[1])
    normal = jnp.stack([cos_polar * cos_azim, cos_polar * sin_azim, sin_polar])
    tan_a = jnp.stack([-sin_azim, cos_azim, jnp.zeros_like(cos_azim)])
    tan_b = jnp.stack([-sin_polar * cos_azim, -sin_polar * sin_azim, cos_polar])
    return (normal, tan_a, tan_b)


def mobility(radius):
    cubed = radius * radius * radius
    linear = 1.0 / cubed
    angular = 2.5 / (cubed * radius * radius)
    return jnp.stack([linear, linear, linear, angular, angular, angular])


def project(trial_n, trial_a, trial_b, coulomb):
    tangent_len = jnp.sqrt(trial_a * trial_a + trial_b * trial_b)
    inside = tangent_len <= coulomb * trial_n
    dead = coulomb * tangent_len <= -trial_n
    cone_level = (trial_n + coulomb * tangent_len) / (1.0 + coulomb * coulomb)
    factor = coulomb * cone_level / jnp.maximum(tangent_len, SMALLEST)
    push_n = jnp.where(inside, trial_n, jnp.where(dead, 0.0, cone_level))
    push_a = jnp.where(inside, trial_a, jnp.where(dead, 0.0, factor * trial_a))
    push_b = jnp.where(inside, trial_b, jnp.where(dead, 0.0, factor * trial_b))
    return jnp.stack([push_n, push_a, push_b])


def listed(velocity, flat_idx, list_len):
    picked = jnp.take(velocity, flat_idx, axis=1).reshape(6, 4, list_len)
    return jnp.transpose(picked, (1, 0, 2))


def assemble(face_parts, corner_parts):
    face_len = face_parts.shape[2]
    widened = jnp.pad(corner_parts, ((0, 0), (0, 0), (0, face_len - corner_parts.shape[2])))
    zeros_cell = jnp.zeros_like(face_parts[0])
    cells = [
        [widened[0], face_parts[0], widened[1]],
        [face_parts[2], zeros_cell, face_parts[3]],
        [widened[2], face_parts[1], widened[3]],
    ]
    return jnp.stack([jnp.stack(line) for line in cells])


def split_grid(padded, corner_len):
    face_parts = jnp.stack([padded[0, 2], padded[4, 2], padded[2, 0], padded[2, 4]])
    corner_parts = jnp.stack(
        [
            padded[0, 0, :, :corner_len],
            padded[0, 4, :, :corner_len],
            padded[4, 0, :, :corner_len],
            padded[4, 4, :, :corner_len],
        ]
    )
    return (face_parts, corner_parts)


def fetch_ghosts(face_parts, corner_parts):
    padded = padded_2(assemble(face_parts, corner_parts), (("gx", 0), ("gy", 1)), 1)
    return split_grid(padded, corner_parts.shape[2])


def return_owed(face_parts, corner_parts):
    padded = padded_2(assemble(face_parts, corner_parts), (("gx", 0), ("gy", 1)), 1)
    return split_grid(padded, corner_parts.shape[2])


def shards(
    free_velocity,
    body_radius,
    face_lists,
    corner_lists,
    owner_body,
    other_body,
    contact_angles,
    contact_arms,
    friction,
    approach,
    start_impulse,
):
    base_velocity = free_velocity[0, 0]
    face_idx = face_lists[0, 0]
    corner_idx = corner_lists[0, 0]
    owner_ids = owner_body[0, 0]
    other_ids = other_body[0, 0]
    arm_pair = contact_arms[0, 0]
    coulomb = friction[0, 0]
    approach_rate = approach[0, 0]
    inverse = mobility(body_radius[0, 0])
    normal, tan_a, tan_b = frames(contact_angles[0, 0])
    own_count = base_velocity.shape[1]
    face_len = face_idx.shape[1]
    corner_len = corner_idx.shape[1]
    contact_count = owner_ids.shape[0]
    corner_base = own_count + 4 * face_len
    extent = corner_base + 4 * corner_len
    arm_near = arm_pair[0] * arm_pair[0] * arm_pair[0]
    arm_far = arm_pair[1] * arm_pair[1] * arm_pair[1]
    relax_step = RELAX / (1.0 / arm_near + 1.0 / arm_far)
    pair_ids = jnp.concatenate([owner_ids, other_ids])
    face_flat = face_idx.reshape(-1)
    corner_flat = corner_idx.reshape(-1)
    shared_ids = jnp.concatenate([face_flat, corner_flat])

    def pulse_of(impulse_now):
        force = impulse_now[0] * normal + impulse_now[1] * tan_a + impulse_now[2] * tan_b
        twist = impulse_now[1] * tan_b - impulse_now[2] * tan_a
        on_owner = jnp.concatenate([force, -arm_pair[0] * twist], axis=0)
        on_other = jnp.concatenate([-force, -arm_pair[1] * twist], axis=0)
        total = jnp.zeros((6, extent), jnp.float32)
        return total.at[:, pair_ids].add(jnp.concatenate([on_owner, on_other], axis=1))

    def settle(pulse):
        own_pulse = pulse[:, :own_count]
        face_parts = jnp.transpose(
            pulse[:, own_count:corner_base].reshape(6, 4, face_len), (1, 0, 2)
        )
        corner_parts = jnp.transpose(
            pulse[:, corner_base:extent].reshape(6, 4, corner_len), (1, 0, 2)
        )
        got_faces, got_corners = return_owed(face_parts, corner_parts)
        received = jnp.concatenate(
            [
                jnp.transpose(got_faces, (1, 0, 2)).reshape(6, 4 * face_len),
                jnp.transpose(got_corners, (1, 0, 2)).reshape(6, 4 * corner_len),
            ],
            axis=1,
        )
        own_pulse = own_pulse.at[:, shared_ids].add(received)
        return base_velocity + inverse * own_pulse

    impulse_now = start_impulse[0, 0]
    velocity = settle(pulse_of(impulse_now))
    for sweep in range(SWEEPS):
        extend_got_faces, extend_got_corners = fetch_ghosts(
            listed(velocity, face_flat, face_len), listed(velocity, corner_flat, corner_len)
        )
        pieces = [
            velocity,
            jnp.transpose(extend_got_faces, (1, 0, 2)).reshape(6, 4 * face_len),
            jnp.transpose(extend_got_corners, (1, 0, 2)).reshape(6, 4 * corner_len),
        ]
        extended = jnp.concatenate(pieces, axis=1)
        both_vel = jnp.take(extended, pair_ids, axis=1)
        near_vel = both_vel[:, :contact_count]
        far_vel = both_vel[:, contact_count:]
        slip_lin = near_vel[:3] - far_vel[:3]
        spin_sum = arm_pair[0] * near_vel[3:] + arm_pair[1] * far_vel[3:]
        normal_rate = jnp.sum(normal * slip_lin, axis=0)
        rate_a = jnp.sum(tan_a * slip_lin, axis=0) - jnp.sum(tan_b * spin_sum, axis=0)
        rate_b = jnp.sum(tan_b * slip_lin, axis=0) + jnp.sum(tan_a * spin_sum, axis=0)
        impulse_now = project(
            impulse_now[0] - relax_step * (normal_rate + approach_rate),
            impulse_now[1] - relax_step * rate_a,
            impulse_now[2] - relax_step * rate_b,
            coulomb,
        )
        velocity = settle(pulse_of(impulse_now))
    return (velocity[None, None], impulse_now[None, None])


def solution(mesh):
    in_specs = (
        P("gx", "gy", None, None),
        P("gx", "gy", None),
        P("gx", "gy", None, None),
        P("gx", "gy", None, None),
        P("gx", "gy", None),
        P("gx", "gy", None),
        P("gx", "gy", None, None),
        P("gx", "gy", None, None),
        P("gx", "gy", None),
        P("gx", "gy", None),
        P("gx", "gy", None, None),
    )
    out_specs = (P("gx", "gy", None, None), P("gx", "gy", None, None))
    return jax.shard_map(shards, mesh=mesh, in_specs=in_specs, out_specs=out_specs, check_vma=False)
```

profile of v0, /device:TPU:6, one launch (start us, length us, event | category | flops | bytes accessed | tf_op | source)
XLA Modules:
  0.0 710.5 jit_solution(2082165379705035366)
XLA Ops:
  9.6 44.7 %scatter_custom_fusion = f32[6,3200]{0,1:T(8,128)S(1)} fusion(s32[8192]{0:T(1024)S(1)} %bitcast.681, f32[8192,6]{1,0:T(8,128)} %copy.275, f32[]{:T(128)} %constant.6.clone.1), kind=kCustom, calls=%fused_computation.40 | custom fusion | flops 49152 | bytes 77312 | tf_op jit(solution)/shard_map/scatter-add | solution.py:139
  66.5 8.0 %collective-permute-start.3 = (f32[5,1,6,256]{3,1,2,0:T(1,128)S(1)}, f32[5,1,6,256]{3,1,2,0:T(1,128)S(1)}, u32[]{:S(2)}, u32[]{:S(2)}) collective-permute-start(f32[5,1,6,256]{3,1,2,0:T(1,128)S(1)} %copy.279), channel_id=1, source_target_pairs={{1,0},{2,1},{3,2},{4,3},{5,4},{6,5},{7,6},{8,7},{9,8},{10,9},{11,1... | collective-permute-start | bytes 92168 | tf_op jit(solution)/shard_map/ppermute | solution.py:21
  78.0 4.5 collective-permute-done.2
  84.5 9.5 %scatter_fusion = f32[6,2048]{0,1:T(8,128)S(1)} fusion(f32[6,2048]{0,1:T(8,128)S(1)} %slice-done, s32[1152]{0:T(1024)S(1)} %fusion.39, f32[1152,6]{1,0:T(8,128)} %copy.282), kind=kCustom, calls=%fused_computation.13 | custom fusion | flops 6912 | bytes 87552 | tf_op jit(solution)/shard_map/scatter-add | solution.py:157
  97.4 5.3 gather_fusion.1
  109.8 4.3 collective-permute-done.5
  116.4 4.0 collective-permute-start.6
  121.0 3.3 collective-permute-done.6
  130.5 29.3 %gather_fusion.2 = f32[8192,6]{1,0:T(8,128)} fusion(f32[6,3200]{0,1:T(8,128)} %pad_maximum_fusion, s32[8192]{0:T(1024)S(1)} %fusion.15), kind=kCustom, calls=%fused_computation.2.clone | custom fusion | bytes 425984 | tf_op jit(solution)/shard_map/jit(_take)/gather | solution.py:172
  159.8 2.9 copy.292
  166.3 45.5 %scatter_custom_fusion.2 = f32[6,3200]{0,1:T(8,128)} fusion(s32[8192]{0:T(1024)} %bitcast.682, f32[8192,6]{1,0:T(8,128)} %copy.293, f32[]{:T(128)} %constant.6.clone.1), kind=kCustom, calls=%fused_computation.38 | custom fusion | flops 49152 | bytes 77312 | tf_op jit(solution)/shard_map/scatter-add | solution.py:139
  213.2 3.1 collective-permute-start.8
  223.8 3.9 collective-permute-start.10
  238.2 9.5 %scatter_fusion.1 = f32[6,2048]{0,1:T(8,128)S(1)} fusion(f32[6,2048]{0,1:T(8,128)S(1)} %slice-done.6, s32[1152]{0:T(1024)S(1)} %fusion.39, f32[1152,6]{1,0:T(8,128)} %copy.300), kind=kCustom, calls=%fused_computation.15 | custom fusion | flops 6912 | bytes 87552 | tf_op jit(solution)/shard_map/scatter-add | solution.py:157
  250.9 5.3 gather_fusion.4
  261.8 3.3 collective-permute-start.12
  271.7 4.3 collective-permute-start.14
  276.7 2.9 collective-permute-done.14
  286.4 29.3 %gather_fusion.5 = f32[8192,6]{1,0:T(8,128)} fusion(f32[6,3200]{0,1:T(8,128)} %pad_maximum_fusion.1, s32[8192]{0:T(1024)S(1)} %fusion.15), kind=kCustom, calls=%fused_computation.9.clone | custom fusion | bytes 425984 | tf_op jit(solution)/shard_map/jit(_take)/gather | solution.py:172
  315.7 2.9 copy.310
  322.4 45.5 %scatter_custom_fusion.4 = f32[6,3200]{0,1:T(8,128)} fusion(s32[8192]{0:T(1024)} %bitcast.683, f32[8192,6]{1,0:T(8,128)} %copy.311, f32[]{:T(128)} %constant.6.clone.1), kind=kCustom, calls=%fused_computation.36 | custom fusion | flops 49152 | bytes 77312 | tf_op jit(solution)/shard_map/scatter-add | solution.py:139
  369.2 3.3 collective-permute-start.16
  379.4 3.9 collective-permute-start.18
  383.4 3.9 collective-permute-done.18
  393.1 9.5 %scatter_fusion.2 = f32[6,2048]{0,1:T(8,128)S(1)} fusion(f32[6,2048]{0,1:T(8,128)S(1)} %slice-done.4, s32[1152]{0:T(1024)S(1)} %fusion.39, f32[1152,6]{1,0:T(8,128)} %copy.318), kind=kCustom, calls=%fused_computation.17 | custom fusion | flops 6912 | bytes 87552 | tf_op jit(solution)/shard_map/scatter-add | solution.py:157
  405.8 5.3 gather_fusion.7
  417.4 3.3 collective-permute-start.20
  427.2 4.1 collective-permute-start.22
  432.0 3.1 collective-permute-done.22
  442.0 29.3 %gather_fusion.8 = f32[8192,6]{1,0:T(8,128)} fusion(f32[6,3200]{0,1:T(8,128)} %pad_maximum_fusion.2, s32[8192]{0:T(1024)S(1)} %fusion.15), kind=kCustom, calls=%fused_computation.10.clone | custom fusion | bytes 425984 | tf_op jit(solution)/shard_map/jit(_take)/gather | solution.py:172
  471.3 2.9 copy.328
  478.0 45.5 %scatter_custom_fusion.6 = f32[6,3200]{0,1:T(8,128)} fusion(s32[8192]{0:T(1024)} %bitcast.684, f32[8192,6]{1,0:T(8,128)} %copy.329, f32[]{:T(128)} %constant.6.clone.1), kind=kCustom, calls=%fused_computation.34 | custom fusion | flops 49152 | bytes 77312 | tf_op jit(solution)/shard_map/scatter-add | solution.py:139
  524.9 3.3 collective-permute-start.24
  530.9 3.3 collective-permute-done.25
  536.1 3.9 collective-permute-start.26
  540.2 3.9 collective-permute-done.26
  548.5 9.5 %scatter_fusion.3 = f32[6,2048]{0,1:T(8,128)S(1)} fusion(f32[6,2048]{0,1:T(8,128)S(1)} %slice-done.2, s32[1152]{0:T(1024)S(1)} %fusion.39, f32[1152,6]{1,0:T(8,128)} %copy.336), kind=kCustom, calls=%fused_computation.19 | custom fusion | flops 6912 | bytes 87552 | tf_op jit(solution)/shard_map/scatter-add | solution.py:157
  561.2 5.3 gather_fusion.10
  572.1 3.3 collective-permute-start.28
  581.9 4.1 collective-permute-start.30
  586.2 3.7 collective-permute-done.30
  596.0 29.3 %gather_fusion.11 = f32[8192,6]{1,0:T(8,128)} fusion(f32[6,3200]{0,1:T(8,128)} %pad_maximum_fusion.3, s32[8192]{0:T(1024)S(1)} %fusion.15), kind=kCustom, calls=%fused_computation.11.clone | custom fusion | bytes 425984 | tf_op jit(solution)/shard_map/jit(_take)/gather | solution.py:172
  625.3 2.9 copy.346
  632.2 45.5 %scatter_custom_fusion.8 = f32[6,3200]{0,1:T(8,128)} fusion(s32[8192]{0:T(1024)} %bitcast.685, f32[8192,6]{1,0:T(8,128)} %copy.347, f32[]{:T(128)} %constant.6.clone.1), kind=kCustom, calls=%fused_computation.32 | custom fusion | flops 49152 | bytes 77312 | tf_op jit(solution)/shard_map/scatter-add | solution.py:139
  679.0 3.4 collective-permute-start.32
  688.3 3.9 collective-permute-start.34
  692.3 3.9 collective-permute-done.34
  697.5 9.5 %scatter_fusion.4 = f32[6,2048]{0,1:T(8,128)S(1)} fusion(f32[6,2048]{0,1:T(8,128)S(1)} %slice-done.7, s32[1152]{0:T(1024)S(1)} %fusion.39, f32[1152,6]{1,0:T(8,128)} %copy.354), kind=kCustom, calls=%fused_computation.21 | custom fusion | flops 6912 | bytes 87552 | tf_op jit(solution)/shard_map/scatter-add | solution.py:157
  (617 shorter events, 182.6 us)
Async XLA Ops:
  9.6 50.8 %copy-start.89 = (s32[1,1,4,32]{3,2,1,0:T(4,128)S(1)}, s32[1,1,4,32]{3,2,1,0:T(4,128)}, u32[]{:S(2)}) copy-start(s32[1,1,4,32]{3,2,1,0:T(4,128)} %param.20) | copy-start | bytes 1540
  9.6 51.5 %copy-start.88 = (f32[1,1,2048]{2,1,0:T(1,128)S(1)}, f32[1,1,2048]{2,1,0:T(1,128)}, u32[]{:S(2)}) copy-start(f32[1,1,2048]{2,1,0:T(1,128)} %param.18) | copy-start | bytes 24580
  9.6 51.6 %copy-start.83 = (s32[1,1,4,256]{3,2,1,0:T(4,128)S(1)}, s32[1,1,4,256]{3,2,1,0:T(4,128)}, u32[]{:S(2)}) copy-start(s32[1,1,4,256]{3,2,1,0:T(4,128)} %param.19) | copy-start | bytes 12292
  56.1 7.3 %collective-permute-start = (f32[1,3,6,256]{3,2,1,0:T(8,128)}, f32[1,3,6,256]{3,2,1,0:T(8,128)}, u32[]{:S(2)}, u32[]{:S(2)}) collective-permute-start(f32[1,3,6,256]{3,2,1,0:T(8,128)} %maximum_bitcast_fusion.11), channel_id=1, source_target_pairs={{0,32},{32,64},{64,96},{96,128},{128,160},{160,192},{192,224},{1,3... | collective-permute-start | bytes 55304 | tf_op jit(solution)/shard_map/ppermute | solution.py:20
  59.1 6.7 collective-permute-start.1
  66.5 11.4 %collective-permute-start.3 = (f32[5,1,6,256]{3,1,2,0:T(1,128)S(1)}, f32[5,1,6,256]{3,1,2,0:T(1,128)S(1)}, u32[]{:S(2)}, u32[]{:S(2)}) collective-permute-start(f32[5,1,6,256]{3,1,2,0:T(1,128)S(1)} %copy.279), channel_id=1, source_target_pairs={{1,0},{2,1},{3,2},{4,3},{5,4},{6,5},{7,6},{8,7},{9,8},{10,9},{11,1... | collective-permute-start | bytes 92168 | tf_op jit(solution)/shard_map/ppermute | solution.py:21
  74.6 7.9 %collective-permute-start.2 = (f32[5,1,6,256]{3,1,2,0:T(1,128)S(1)}, f32[5,1,6,256]{3,1,2,0:T(1,128)S(1)}, u32[]{:S(2)}, u32[]{:S(2)}) collective-permute-start(f32[5,1,6,256]{3,1,2,0:T(1,128)S(1)} %copy.278), channel_id=1, source_target_pairs={{0,1},{1,2},{2,3},{3,4},{4,5},{5,6},{6,7},{7,8},{8,9},{9,10},{10,1... | collective-permute-start | bytes 92168 | tf_op jit(solution)/shard_map/ppermute | solution.py:20
  106.0 3.7 collective-permute-start.4
  108.4 5.8 collective-permute-start.5
  114.2 6.7 collective-permute-start.7
  116.4 7.9 %collective-permute-start.6 = (f32[5,1,6,256]{3,1,2,0:T(1,128)S(1)}, f32[5,1,6,256]{3,1,2,0:T(1,128)S(1)}, u32[]{:S(2)}, u32[]{:S(2)}) collective-permute-start(f32[5,1,6,256]{3,1,2,0:T(1,128)S(1)} %copy.286), channel_id=1, source_target_pairs={{0,1},{1,2},{2,3},{3,4},{4,5},{5,6},{6,7},{7,8},{8,9},{9,10},{10,1... | collective-permute-start | bytes 92168 | tf_op jit(solution)/shard_map/ppermute | solution.py:20
  213.2 6.0 collective-permute-start.8
  217.7 4.1 collective-permute-start.9
  221.8 7.1 %collective-permute-start.11 = (f32[5,1,6,256]{3,1,2,0:T(1,128)S(1)}, f32[5,1,6,256]{3,1,2,0:T(1,128)S(1)}, u32[]{:S(2)}, u32[]{:S(2)}) collective-permute-start(f32[5,1,6,256]{3,1,2,0:T(1,128)S(1)} %copy.297), channel_id=1, source_target_pairs={{1,0},{2,1},{3,2},{4,3},{5,4},{6,5},{7,6},{8,7},{9,8},{10,9},{11,1... | collective-permute-start | bytes 92168 | tf_op jit(solution)/shard_map/ppermute | solution.py:21
  223.8 7.9 %collective-permute-start.10 = (f32[5,1,6,256]{3,1,2,0:T(1,128)S(1)}, f32[5,1,6,256]{3,1,2,0:T(1,128)S(1)}, u32[]{:S(2)}, u32[]{:S(2)}) collective-permute-start(f32[5,1,6,256]{3,1,2,0:T(1,128)S(1)} %copy.296), channel_id=1, source_target_pairs={{0,1},{1,2},{2,3},{3,4},{4,5},{5,6},{6,7},{7,8},{8,9},{9,10},{10,1... | collective-permute-start | bytes 92168 | tf_op jit(solution)/shard_map/ppermute | solution.py:20
  261.8 5.3 collective-permute-start.12
  265.9 3.7 collective-permute-start.13
  269.7 6.9 collective-permute-start.15
  271.7 7.9 %collective-permute-start.14 = (f32[5,1,6,256]{3,1,2,0:T(1,128)S(1)}, f32[5,1,6,256]{3,1,2,0:T(1,128)S(1)}, u32[]{:S(2)}, u32[]{:S(2)}) collective-permute-start(f32[5,1,6,256]{3,1,2,0:T(1,128)S(1)} %copy.304), channel_id=1, source_target_pairs={{0,1},{1,2},{2,3},{3,4},{4,5},{5,6},{6,7},{7,8},{8,9},{9,10},{10,1... | collective-permute-start | bytes 92168 | tf_op jit(solution)/shard_map/ppermute | solution.py:20
  369.2 5.6 collective-permute-start.16
  373.4 3.9 collective-permute-start.17
  377.4 6.0 collective-permute-start.19
  379.4 7.9 %collective-permute-start.18 = (f32[5,1,6,256]{3,1,2,0:T(1,128)S(1)}, f32[5,1,6,256]{3,1,2,0:T(1,128)S(1)}, u32[]{:S(2)}, u32[]{:S(2)}) collective-permute-start(f32[5,1,6,256]{3,1,2,0:T(1,128)S(1)} %copy.314), channel_id=1, source_target_pairs={{0,1},{1,2},{2,3},{3,4},{4,5},{5,6},{6,7},{7,8},{8,9},{9,10},{10,1... | collective-permute-start | bytes 92168 | tf_op jit(solution)/shard_map/ppermute | solution.py:20
  417.4 5.3 collective-permute-start.20
  421.5 3.7 collective-permute-start.21
  425.3 6.7 collective-permute-start.23
  427.2 7.9 %collective-permute-start.22 = (f32[5,1,6,256]{3,1,2,0:T(1,128)S(1)}, f32[5,1,6,256]{3,1,2,0:T(1,128)S(1)}, u32[]{:S(2)}, u32[]{:S(2)}) collective-permute-start(f32[5,1,6,256]{3,1,2,0:T(1,128)S(1)} %copy.322), channel_id=1, source_target_pairs={{0,1},{1,2},{2,3},{3,4},{4,5},{5,6},{6,7},{7,8},{8,9},{9,10},{10,1... | collective-permute-start | bytes 92168 | tf_op jit(solution)/shard_map/ppermute | solution.py:20
  478.0 50.2 %copy-start.8 = (f32[1,1,3,4096]{3,1,2,0:T(1,128)S(1)}, f32[1,1,3,4096]{3,1,2,0:T(1,128)}, u32[]{:S(2)}) copy-start(f32[1,1,3,4096]{3,1,2,0:T(1,128)} %param.27) | copy-start | bytes 147460
  478.0 50.2 %copy-start.13 = (f32[4096]{0:T(1024)S(1)}, f32[4096]{0:T(1024)}, u32[]{:S(2)}) copy-start(f32[4096]{0:T(1024)} %copy-done.11) | copy-start | bytes 49156
  478.0 50.2 %copy-start.27 = (f32[4096]{0:T(1024)S(1)}, f32[4096]{0:T(1024)}, u32[]{:S(2)}) copy-start(f32[4096]{0:T(1024)} %copy-done.26) | copy-start | bytes 49156
  478.0 50.2 %copy-start.29 = (f32[4096]{0:T(1024)S(1)}, f32[4096]{0:T(1024)}, u32[]{:S(2)}) copy-start(f32[4096]{0:T(1024)} %copy-done.28) | copy-start | bytes 49156
  478.0 50.2 %copy-start.61 = (f32[1,4096]{1,0:T(1,128)S(1)}, f32[1,4096]{1,0:T(1,128)}, u32[]{:S(2)}) copy-start(f32[1,4096]{1,0:T(1,128)} %get-tuple-element.58) | copy-start | bytes 49156
  478.0 50.2 %copy-start.62 = (f32[1,4096]{1,0:T(1,128)S(1)}, f32[1,4096]{1,0:T(1,128)}, u32[]{:S(2)}) copy-start(f32[1,4096]{1,0:T(1,128)} %get-tuple-element.59) | copy-start | bytes 49156
  478.0 50.2 %copy-start.63 = (pred[1,4096]{1,0:T(4,128)(4,1)S(1)}, pred[1,4096]{1,0:T(4,128)(4,1)}, u32[]{:S(2)}) copy-start(pred[1,4096]{1,0:T(4,128)(4,1)} %get-tuple-element.60) | copy-start | bytes 12292
  478.0 50.2 %copy-start.64 = (pred[1,4096]{1,0:T(4,128)(4,1)S(1)}, pred[1,4096]{1,0:T(4,128)(4,1)}, u32[]{:S(2)}) copy-start(pred[1,4096]{1,0:T(4,128)(4,1)} %get-tuple-element.61) | copy-start | bytes 12292
  478.0 50.2 %copy-start.65 = (f32[1,4096]{1,0:T(1,128)S(1)}, f32[1,4096]{1,0:T(1,128)}, u32[]{:S(2)}) copy-start(f32[1,4096]{1,0:T(1,128)} %get-tuple-element.62) | copy-start | bytes 49156
  524.9 5.8 collective-permute-start.24
  529.3 4.8 collective-permute-start.25
  534.2 6.0 collective-permute-start.27
  536.1 7.9 %collective-permute-start.26 = (f32[5,1,6,256]{3,1,2,0:T(1,128)S(1)}, f32[5,1,6,256]{3,1,2,0:T(1,128)S(1)}, u32[]{:S(2)}, u32[]{:S(2)}) collective-permute-start(f32[5,1,6,256]{3,1,2,0:T(1,128)S(1)} %copy.332), channel_id=1, source_target_pairs={{0,1},{1,2},{2,3},{3,4},{4,5},{5,6},{6,7},{7,8},{8,9},{9,10},{10,1... | collective-permute-start | bytes 92168 | tf_op jit(solution)/shard_map/ppermute | solution.py:20
  572.1 5.3 collective-permute-start.28
  576.2 3.7 collective-permute-start.29
  580.0 6.2 collective-permute-start.31
  581.9 7.9 %collective-permute-start.30 = (f32[5,1,6,256]{3,1,2,0:T(1,128)S(1)}, f32[5,1,6,256]{3,1,2,0:T(1,128)S(1)}, u32[]{:S(2)}, u32[]{:S(2)}) collective-permute-start(f32[5,1,6,256]{3,1,2,0:T(1,128)S(1)} %copy.340), channel_id=1, source_target_pairs={{0,1},{1,2},{2,3},{3,4},{4,5},{5,6},{6,7},{7,8},{8,9},{9,10},{10,1... | collective-permute-start | bytes 92168 | tf_op jit(solution)/shard_map/ppermute | solution.py:20
  679.0 6.2 collective-permute-start.32
  682.5 3.8 collective-permute-start.33
  686.3 6.0 collective-permute-start.35
  688.3 7.9 %collective-permute-start.34 = (f32[5,1,6,256]{3,1,2,0:T(1,128)S(1)}, f32[5,1,6,256]{3,1,2,0:T(1,128)S(1)}, u32[]{:S(2)}, u32[]{:S(2)}) collective-permute-start(f32[5,1,6,256]{3,1,2,0:T(1,128)S(1)} %copy.350), channel_id=1, source_target_pairs={{0,1},{1,2},{2,3},{3,4},{4,5},{5,6},{6,7},{7,8},{8,9},{9,10},{10,1... | collective-permute-start | bytes 92168 | tf_op jit(solution)/shard_map/ppermute | solution.py:20
  (103 other events, 847.1 us)
where the time goes:
time: 724 us; the launch traced here: 711 us
  other arithmetic  330 us (46%)
  local copies, waits for them, and re-layouts  233 us (32%)
  starting transfers between devices  97.5 us (13%)
  waiting for transfers between devices  46.1 us (6%)
    scatter-add x5, other arithmetic, pulse_of(): total.at[:, pair_ids].add(jnp.concatenate([on_owner, on_other], axis=1))  227 us
    gather x8, local copies, waits for them, and re-layouts, shards(): both_vel = jnp.take(extended, pair_ids, axis=1)  129 us
    ppermute x18, starting transfers between devices, padded_2(): before = lax.ppermute(last, axis, up)  62 us
    scatter-add x5, other arithmetic, settle(): own_pulse = own_pulse.at[:, shared_ids].add(received)  47.7 us
    ppermute x18, starting transfers between devices, padded_2(): after = lax.ppermute(first, axis, down)  35.5 us
    ppermute x18, waiting for transfers between devices, padded_2(): before = lax.ppermute(last, axis, up)  31.9 us
    gather x8, local copies, waits for them, and re-layouts, listed(): picked = jnp.take(velocity, flat_idx, axis=1).reshape(6, 4, list_len)  29 us
    another operation x54, local copies, waits for them, and re-layouts, split_grid(): jnp.stack([padded[0, 2], padded[4, 2], padded[2, 0], padded[2, 4]])  14.9 us
  transfers between devices with their start and end apart: 36, of which 17 were waited for; matrix products, arithmetic and copies ran while one was open for 3% of the time, Pallas kernels for 0%

commit v1 on v0

v1 whole, which is shorter than its diff:
```python
import jax
import jax.numpy as jnp
from jax import lax
from jax.experimental import pallas as pl
from jax.experimental.pallas import tpu as pltpu
from jax.sharding import PartitionSpec as P

SWEEPS = 4
RELAX = 0.25
SMALLEST = 1e-20

BODY = 2048
FACE = 256
CORNER = 32
CONTACTS = 4096
ROWS = CONTACTS // 128
LISTED = 4 * FACE + 4 * CORNER
LIST_ROWS = LISTED // 128
OWN_TILES = BODY // 128
WIDE = 256
OWN_WIDE = BODY // WIDE
ALL_WIDE = 14
MESSAGE = FACE + 128

F32 = jnp.float32
BF16 = jnp.bfloat16
I32 = jnp.int32

PLANES = (
    "n0", "n1", "n2", "a0", "a1", "b0", "b1", "b2",
    "arm0", "arm1", "relax", "mu", "bias",
)
PLANE = {name: place for place, name in enumerate(PLANES)}


def lanes_of(table, lane):
    numbers = lax.GatherDimensionNumbers(
        offset_dims=(),
        collapsed_slice_dims=(1,),
        start_index_map=(1,),
        operand_batching_dims=(0,),
        start_indices_batching_dims=(0,),
    )
    return lax.gather(
        table, lane[..., None], numbers, (1, 1),
        mode=lax.GatherScatterMode.PROMISE_IN_BOUNDS,
    )


def iota(shape, dim):
    return lax.broadcasted_iota(I32, shape, dim)


def halves(values):
    high = values.astype(BF16).astype(F32)
    return high, values - high


def plane(ref, number):
    return ref[number * ROWS:(number + 1) * ROWS, :]


def spread(ref, row, high_row, parts, blocks, column):
    picks = [high_row == block for block in range(blocks)]
    for part, value in enumerate(parts):
        zero = jnp.zeros_like(value)
        for pair in range(blocks // 2):
            both = jnp.concatenate(
                [
                    jnp.where(picks[2 * pair], value, zero),
                    jnp.where(picks[2 * pair + 1], value, zero),
                ],
                axis=0,
            )
            start = part * blocks * 8 + pair * 16
            ref[start:start + 16, column:column + 128] = both.astype(BF16)


def lane_hot(ref, low, rows):
    turned = jnp.transpose(low)
    along = iota((128, WIDE), 1)
    for row in range(rows):
        hot = jnp.broadcast_to(turned[:, row:row + 1], (128, WIDE)) == along
        ref[row * 128:(row + 1) * 128, :] = jnp.where(hot, 1.0, 0.0).astype(BF16)


def scatter_contacts(impulse, table, high, left_near, left_far, moved):
    p0, p1, p2 = impulse
    get = lambda name: plane(table, PLANE[name])
    a0, a1 = get("a0"), get("a1")
    b0, b1, b2 = get("b0"), get("b1"), get("b2")
    force = (
        p0 * get("n0") + p1 * a0 + p2 * b0,
        p0 * get("n1") + p1 * a1 + p2 * b1,
        p0 * get("n2") + p2 * b2,
    )
    twist = (p1 * b0 - p2 * a0, p1 * b1 - p2 * a1, p1 * b2)
    arm0, arm1 = -get("arm0"), -get("arm1")
    for comp in range(3):
        moved[0, pl.ds(comp, ROWS, stride=8), :] = force[comp]
        moved[1, pl.ds(comp, ROWS, stride=8), :] = -force[comp]
        moved[0, pl.ds(comp + 3, ROWS, stride=8), :] = arm0 * twist[comp]
        moved[1, pl.ds(comp + 3, ROWS, stride=8), :] = arm1 * twist[comp]
    for comp in (6, 7):
        moved[0, pl.ds(comp, ROWS, stride=8), :] = jnp.zeros((ROWS, 128), F32)
        moved[1, pl.ds(comp, ROWS, stride=8), :] = jnp.zeros((ROWS, 128), F32)
    for row in range(ROWS):
        near = moved[0, row * 8:(row + 1) * 8, :]
        far = moved[1, row * 8:(row + 1) * 8, :]
        spread(left_near, row, high[row:row + 1, :], halves(near), OWN_WIDE, row * 128)
        spread(
            left_far, row, high[ROWS + row:ROWS + row + 1, :], halves(far), ALL_WIDE, row * 128
        )


def pulses(impulse, table, high, hot_near, hot_far, own_out, up, down, left, right, scratch):
    left_near, left_far, moved = scratch
    scatter_contacts(impulse, table, high, left_near, left_far, moved)
    near = jnp.dot(left_near[...], hot_near[...], preferred_element_type=F32)
    far = jnp.dot(left_far[...], hot_far[...], preferred_element_type=F32)
    near = near[:OWN_WIDE * 8] + near[OWN_WIDE * 8:]
    far = far[:ALL_WIDE * 8] + far[ALL_WIDE * 8:]
    for block in range(OWN_WIDE):
        rows = slice(block * 8, block * 8 + 8)
        own_out[:, block * WIDE:(block + 1) * WIDE] = near[rows] + far[rows]
    ghost = [far[block * 8:block * 8 + 8] for block in range(OWN_WIDE, OWN_WIDE + 5)]
    send(ghost[0], ghost[1], ghost[2], ghost[3], ghost[4][:, :128], up, down, left, right)


def send(face0, face1, face2, face3, corners, up, down, left, right):
    slot = iota((8, 128), 1) // CORNER
    to_down = (slot == 0) | (slot == 2)
    up[:, :FACE] = face0
    up[:, FACE:] = jnp.where(to_down, 0.0, corners)
    down[:, :FACE] = face1
    down[:, FACE:] = jnp.where(to_down, corners, 0.0)
    left[...] = face2
    right[...] = face3


def prepare(
    angles, arms, mu, bias, impulse, owner, other, radius, faces, corners,
    table, places, high, inverse, impulse_out, hot_near, hot_far, hot_list, list_places,
    own_out, up, down, left, right,
    flat, left_near, left_far, moved,
):
    for row in range(ROWS):
        cut = slice(row * 128, (row + 1) * 128)
        flat[pl.ds(row, 2, stride=ROWS), :] = angles[:, cut]
        flat[pl.ds(2 * ROWS + row, 2, stride=ROWS), :] = arms[:, cut]
        flat[pl.ds(4 * ROWS + row, 3, stride=ROWS), :] = impulse[:, cut]
    polar, azim = plane(flat, 0), plane(flat, 1)
    arm0, arm1 = plane(flat, 2), plane(flat, 3)
    impulse_now = [plane(flat, 4 + comp) for comp in range(3)]
    cos_polar, sin_polar = jnp.cos(polar), jnp.sin(polar)
    cos_azim, sin_azim = jnp.cos(azim), jnp.sin(azim)
    cubed0 = arm0 * arm0 * arm0
    cubed1 = arm1 * arm1 * arm1
    values = {
        "n0": cos_polar * cos_azim, "n1": cos_polar * sin_azim, "n2": sin_polar,
        "a0": -sin_azim, "a1": cos_azim,
        "b0": -sin_polar * cos_azim, "b1": -sin_polar * sin_azim, "b2": cos_polar,
        "arm0": arm0, "arm1": arm1,
        "relax": RELAX / (1.0 / cubed0 + 1.0 / cubed1),
        "mu": mu[...], "bias": bias[...],
    }
    for name, value in values.items():
        number = PLANE[name]
        table[number * ROWS:(number + 1) * ROWS, :] = value
    for comp in range(3):
        impulse_out[comp * ROWS:(comp + 1) * ROWS, :] = impulse_now[comp]

    near_id = owner[...]
    far_id = other[...]
    extra = far_id - (BODY + 4 * FACE)
    block = extra >> 5
    slot = ((block & 1) << 1) | (block >> 1)
    in_block = extra & (CORNER - 1)
    is_corner = extra >= 0
    places[:ROWS, :] = near_id >> 7
    places[ROWS:2 * ROWS, :] = near_id & 127
    places[2 * ROWS:3 * ROWS, :] = far_id >> 7
    places[3 * ROWS:, :] = jnp.where(is_corner, slot * CORNER + in_block, far_id & 127)
    high[:ROWS, :] = near_id >> 8
    high[ROWS:, :] = far_id >> 8
    lane_hot(hot_near, near_id & 255, ROWS)
    lane_hot(
        hot_far, jnp.where(is_corner, (3 - slot) * CORNER + in_block, far_id & 255), ROWS
    )

    for number in range(4):
        for part in range(2):
            row = number * 2 + part
            list_places[row:row + 1, :] = faces[number:number + 1, part * 128:(part + 1) * 128]
    for place, number in enumerate((0, 2, 1, 3)):
        list_places[8:9, place * CORNER:(place + 1) * CORNER] = corners[number:number + 1, :]
    for place, number in enumerate((3, 1, 2, 0)):
        list_places[9:10, place * CORNER:(place + 1) * CORNER] = corners[number:number + 1, :]
    list_places[10:, :] = jnp.zeros((6, 128), I32)
    lane_hot(hot_list, list_places[...] & 255, LIST_ROWS)

    size = radius[...]
    cubed = size * size * size
    linear = 1.0 / cubed
    angular = 2.5 / (cubed * size * size)
    inverse[...] = jnp.where(iota((8, BODY), 0) < 3, linear, angular)
    pulses(
        impulse_now, table, high, hot_near, hot_far, own_out, up, down, left, right,
        (left_near, left_far, moved),
    )


def forward(flags, from_up, from_down, left, right, to_left, to_right):
    corners = masked(flags, 0, from_up[:, FACE:]) + masked(flags, 1, from_down[:, FACE:])
    to_left[:, :FACE] = left[...]
    to_right[:, :FACE] = right[...]
    to_left[:, FACE:] = corners
    to_right[:, FACE:] = corners


def masked(flags, number, value):
    return jnp.where(flags[number] > 0, value, jnp.zeros_like(value))


def received_tiles(flags, from_up, from_down, from_left, from_right):
    tiles = []
    for number, ref in enumerate((from_up, from_down, from_left, from_right)):
        for part in range(2):
            tiles.append(masked(flags, number, ref[:, part * 128:(part + 1) * 128]))
    early = iota((8, 128), 1) < 2 * CORNER
    tiles.append(
        jnp.where(
            early, masked(flags, 2, from_left[:, FACE:]), masked(flags, 3, from_right[:, FACE:])
        )
    )
    return tiles


def settled(flags, own, inverse, base, list_places, hot_list, from_up, from_down, from_left, from_right, left_list):
    tiles = received_tiles(flags, from_up, from_down, from_left, from_right)
    for row, tile in enumerate(tiles):
        high_row = list_places[row:row + 1, :] >> 8
        spread(left_list, row, high_row, halves(tile), OWN_WIDE, row * 128)
    added = jnp.dot(left_list[...], hot_list[...], preferred_element_type=F32)
    added = added[:OWN_WIDE * 8] + added[OWN_WIDE * 8:]
    blocks = []
    for block in range(OWN_WIDE):
        cut = slice(block * WIDE, (block + 1) * WIDE)
        total = own[:6, cut] + added[block * 8:block * 8 + 6]
        blocks.append(base[:, cut] + inverse[:6, cut] * total)
    return blocks


def settle(
    flags, own, inverse, base, list_places, hot_list, from_up, from_down, from_left, from_right,
    velocity, up, down, left, right, left_list,
):
    blocks = settled(
        flags, own, inverse, base, list_places, hot_list,
        from_up, from_down, from_left, from_right, left_list,
    )
    zero = jnp.zeros((2, WIDE), F32)
    for block, value in enumerate(blocks):
        velocity[:, block * WIDE:(block + 1) * WIDE] = jnp.concatenate([value, zero], axis=0)
    found = []
    for row in (0, 1, 2, 3, 4, 5, 6, 7, 9):
        entry = jnp.broadcast_to(list_places[row:row + 1, :], (8, 128))
        tile_id, lane = entry >> 7, entry & 127
        total = jnp.zeros((8, 128), F32)
        for tile in range(OWN_TILES):
            table = velocity[:, tile * 128:(tile + 1) * 128]
            total = jnp.where(tile_id == tile, lanes_of(table, lane), total)
        found.append(total)
    face = [jnp.concatenate(found[2 * k:2 * k + 2], axis=1) for k in range(4)]
    send(*face, found[8], up, down, left, right)


def settle_last(
    flags, own, inverse, base, list_places, hot_list, from_up, from_down, from_left, from_right,
    velocity, left_list,
):
    blocks = settled(
        flags, own, inverse, base, list_places, hot_list,
        from_up, from_down, from_left, from_right, left_list,
    )
    for block, value in enumerate(blocks):
        velocity[:, block * WIDE:(block + 1) * WIDE] = value


def pick(tables, tile_id, lane, firsts):
    totals = [jnp.zeros((ROWS, 128), F32) for _ in range(6)]
    for tile, table in zip(firsts, tables):
        here = tile_id == tile
        for comp in range(6):
            row = jnp.broadcast_to(table[comp:comp + 1, :], (ROWS, 128))
            totals[comp] = jnp.where(here, lanes_of(row, lane), totals[comp])
    return totals


def solved(flags, velocity, table, places, impulse, from_up, from_down, from_left, from_right):
    own_tables = [velocity[:, tile * 128:(tile + 1) * 128] for tile in range(OWN_TILES)]
    ghosts = received_tiles(flags, from_up, from_down, from_left, from_right)
    near = pick(own_tables, places[:ROWS, :], places[ROWS:2 * ROWS, :], range(OWN_TILES))
    far = pick(
        own_tables + ghosts, places[2 * ROWS:3 * ROWS, :], places[3 * ROWS:, :],
        range(OWN_TILES + 9),
    )
    get = lambda name: plane(table, PLANE[name])
    n0, n1, n2 = get("n0"), get("n1"), get("n2")
    a0, a1 = get("a0"), get("a1")
    b0, b1, b2 = get("b0"), get("b1"), get("b2")
    arm0, arm1, relax, mu = get("arm0"), get("arm1"), get("relax"), get("mu")
    w0, w1, w2 = [near[c] - far[c] for c in range(3)]
    s0, s1, s2 = [arm0 * near[c] + arm1 * far[c] for c in range(3, 6)]
    rate_n = n0 * w0 + n1 * w1 + n2 * w2
    rate_a = (a0 * w0 + a1 * w1) - (b0 * s0 + b1 * s1 + b2 * s2)
    rate_b = (b0 * w0 + b1 * w1 + b2 * w2) + (a0 * s0 + a1 * s1)
    trial_n = plane(impulse, 0) - relax * (rate_n + get("bias"))
    trial_a = plane(impulse, 1) - relax * rate_a
    trial_b = plane(impulse, 2) - relax * rate_b
    length = jnp.sqrt(trial_a * trial_a + trial_b * trial_b)
    inside = length <= mu * trial_n
    dead = mu * length <= -trial_n
    level = (trial_n + mu * length) / (1.0 + mu * mu)
    factor = mu * level / jnp.maximum(length, SMALLEST)
    choose = lambda kept, cone: jnp.where(inside, kept, jnp.where(dead, 0.0, cone))
    return [
        choose(trial_n, level), choose(trial_a, factor * trial_a), choose(trial_b, factor * trial_b)
    ]


def sweep(
    flags, velocity, table, places, high, hot_near, hot_far, impulse,
    from_up, from_down, from_left, from_right,
    impulse_out, own_out, up, down, left, right,
    left_near, left_far, moved,
):
    fresh = solved(
        flags, velocity, table, places, impulse, from_up, from_down, from_left, from_right
    )
    for comp in range(3):
        impulse_out[comp * ROWS:(comp + 1) * ROWS, :] = fresh[comp]
    pulses(
        fresh, table, high, hot_near, hot_far, own_out, up, down, left, right,
        (left_near, left_far, moved),
    )


def shape(*dims, kind=F32):
    return jax.ShapeDtypeStruct(dims, kind)


SENDS = (shape(8, MESSAGE), shape(8, MESSAGE), shape(8, FACE), shape(8, FACE))
LEFTS = (
    pltpu.VMEM((2 * OWN_WIDE * 8, CONTACTS), BF16),
    pltpu.VMEM((2 * ALL_WIDE * 8, CONTACTS), BF16),
    pltpu.VMEM((2, ROWS * 8, 128), F32),
)
LEFT_LIST = pltpu.VMEM((2 * OWN_WIDE * 8, LISTED), BF16)


def call(body, outs, scratch, flagged, *operands):
    vmem = pl.BlockSpec(memory_space=pltpu.VMEM)
    specs = [vmem] * len(operands)
    if flagged:
        specs[0] = pl.BlockSpec(memory_space=pltpu.SMEM)
    return pl.pallas_call(
        body,
        out_shape=outs,
        in_specs=specs,
        out_specs=[vmem] * len(outs),
        scratch_shapes=scratch,
        compiler_params=pltpu.CompilerParams(vmem_limit_bytes=24 * 1024 * 1024),
    )(*operands)


def ring(value, axis, step):
    size = lax.axis_size(axis)
    return lax.ppermute(value, axis, [(i, (i + step) % size) for i in range(size)])


def exchange(flags, up, down, left, right):
    from_up = ring(down, "gx", 1)
    from_down = ring(up, "gx", -1)
    to_left, to_right = call(
        forward, (shape(8, MESSAGE), shape(8, MESSAGE)), (), True,
        flags, from_up, from_down, left, right,
    )
    from_left = ring(to_right, "gy", 1)
    from_right = ring(to_left, "gy", -1)
    return from_up, from_down, from_left, from_right


def shards(
    free_velocity, body_radius, face_lists, corner_lists, owner_body, other_body,
    contact_angles, contact_arms, friction, approach, start_impulse,
):
    base = free_velocity[0, 0]
    row_at, row_count = lax.axis_index("gx"), lax.axis_size("gx")
    col_at, col_count = lax.axis_index("gy"), lax.axis_size("gy")
    flags = jnp.stack(
        [row_at > 0, row_at < row_count - 1, col_at > 0, col_at < col_count - 1]
    ).astype(I32)
    in_rows = lambda value: value[0, 0].reshape(ROWS, 128)
    (
        table, places, high, inverse, impulse, hot_near, hot_far, hot_list, list_places,
        own, up, down, left, right,
    ) = call(
        prepare,
        (
            shape(len(PLANES) * ROWS, 128),
            shape(4 * ROWS, 128, kind=I32),
            shape(2 * ROWS, 128, kind=I32),
            shape(8, BODY),
            shape(3 * ROWS, 128),
            shape(CONTACTS, WIDE, kind=BF16),
            shape(CONTACTS, WIDE, kind=BF16),
            shape(LISTED, WIDE, kind=BF16),
            shape(16, 128, kind=I32),
            shape(8, BODY),
        ) + SENDS,
        (pltpu.VMEM((7 * ROWS, 128), F32),) + LEFTS,
        False,
        contact_angles[0, 0], contact_arms[0, 0], in_rows(friction), in_rows(approach),
        start_impulse[0, 0], in_rows(owner_body), in_rows(other_body),
        body_radius[0], face_lists[0, 0], corner_lists[0, 0],
    )
    for number in range(SWEEPS + 1):
        got = exchange(flags, up, down, left, right)
        fixed = (flags, own, inverse, base, list_places, hot_list)
        if number == SWEEPS:
            (velocity,) = call(
                settle_last, (shape(6, BODY),), (LEFT_LIST,), True, *fixed, *got
            )
            break
        velocity, up, down, left, right = call(
            settle, (shape(8, BODY),) + SENDS, (LEFT_LIST,), True, *fixed, *got
        )
        got = exchange(flags, up, down, left, right)
        impulse, own, up, down, left, right = call(
            sweep, (shape(3 * ROWS, 128), shape(8, BODY)) + SENDS, LEFTS, True,
            flags, velocity, table, places, high, hot_near, hot_far, impulse, *got,
        )
    return velocity[None, None], impulse.reshape(1, 1, 3, CONTACTS)


def solution(mesh):
    in_specs = (
        P("gx", "gy", None, None),
        P("gx", "gy", None),
        P("gx", "gy", None, None),
        P("gx", "gy", None, None),
        P("gx", "gy", None),
        P("gx", "gy", None),
        P("gx", "gy", None, None),
        P("gx", "gy", None, None),
        P("gx", "gy", None),
        P("gx", "gy", None),
        P("gx", "gy", None, None),
    )
    out_specs = (P("gx", "gy", None, None), P("gx", "gy", None, None))
    return jax.shard_map(shards, mesh=mesh, in_specs=in_specs, out_specs=out_specs, check_vma=False)
```

time: 724 us -> 149 us (0.21)
  the two profiles are of different devices: /device:TPU:6 before, /device:TPU:25 now
where the time goes in v1:
time: 149 us; the launch traced here: 148 us
  starting transfers between devices  58.9 us (40%)
  waiting for transfers between devices  46.7 us (31%)
  Pallas kernels  29.6 us (20%)
  local copies, waits for them, and re-layouts  11.7 us (8%)
    ppermute x36, starting transfers between devices, ring(): lax.ppermute(value, axis, [(i, (i + step) % size) for i in range(size)])  58.9 us
    ppermute x36, waiting for transfers between devices, ring(): lax.ppermute(value, axis, [(i, (i + step) % size) for i in range(size)])  46.7 us
    pallas_call x19, Pallas kernels, call(): pl.pallas_call(body, out_shape=outs, in_specs=specs, out_specs=[vmem] * l...  29.6 us
    unnamed x27, local copies, waits for them, and re-layouts  11.7 us
  transfers between devices with their start and end apart: 36, of which 28 were waited for; matrix products, arithmetic and copies ran while one was open for 1% of the time, Pallas kernels for 0%

profile of v1, /device:TPU:25, one launch (start us, length us, event | category | flops | bytes accessed | tf_op | source)
XLA Modules:
  0.0 147.9 jit_solution(17458577694302903857)
XLA Ops:
  0.6 0.8 copy.22
  7.9 2.9 %shard_map.122 = (f32[416,128]{1,0:T(8,128)S(1)}, s32[128,128]{1,0:T(8,128)S(1)}, s32[64,128]{1,0:T(8,128)S(1)}, f32[8,2048]{1,0:T(8,128)S(1)}, f32[96,128]{1,0:...) custom-call(f32[2,4096]{1,0:T(2,128)S(1)} %bitcast.28, ...), custom_call_target="tpu_custom_call" | custom-call | tf_op jit(solution)/shard_map/pallas_call | solution.py:367
  10.8 1.3 copy-done
  12.2 2.2 %collective-permute-start = (f32[8,384]{1,0:T(8,128)S(1)}, f32[8,384]{1,0:T(8,128)S(1)}, u32[]{:S(2)}, u32[]{:S(2)}) collective-permute-start(f32[8,384]{1,0:T(8,128)S(1)} %get-tuple-element.82), channel_id=1, source_target_pairs={{0,32},{32,64},{64,96},{96,128},{128,160},{160,192},{192,224},{224... | collective-permute-start | bytes 36872 | tf_op jit(solution)/shard_map/ppermute | solution.py:379
  15.2 3.5 %collective-permute-done.1.from_down = f32[8,384]{1,0:T(8,128)S(1)} collective-permute-done((f32[8,384]{1,0:T(8,128)S(1)}, f32[8,384]{1,0:T(8,128)S(1)}, u32[]{:S(2)}, u32[]{:S(2)}) %collective-permute-start.1) | collective-permute-done | bytes 12320 | tf_op jit(solution)/shard_map/ppermute | solution.py:379
  19.4 6.1 %collective-permute-start.3 = (f32[8,384]{1,0:T(8,128)S(1)}, f32[8,384]{1,0:T(8,128)S(1)}, u32[]{:S(2)}, u32[]{:S(2)}) collective-permute-start(f32[8,384]{1,0:T(8,128)S(1)} %get-tuple-element.87), channel_id=1, source_target_pairs={{0,31},{1,0},{2,1},{3,2},{4,3},{5,4},{6,5},{7,6},{8,7},{9,8},{10,9... | collective-permute-start | bytes 36872 | tf_op jit(solution)/shard_map/ppermute | solution.py:379
  26.5 1.2 shard_map.124
  27.7 0.9 collective-permute-start.4
  28.6 0.8 collective-permute-done.4.from_up
  29.4 3.5 %collective-permute-done.5.from_down = f32[8,384]{1,0:T(8,128)S(1)} collective-permute-done((f32[8,384]{1,0:T(8,128)S(1)}, f32[8,384]{1,0:T(8,128)S(1)}, u32[]{:S(2)}, u32[]{:S(2)}) %collective-permute-start.5) | collective-permute-done | bytes 12320 | tf_op jit(solution)/shard_map/ppermute | solution.py:379
  33.6 5.2 %collective-permute-start.7 = (f32[8,384]{1,0:T(8,128)S(1)}, f32[8,384]{1,0:T(8,128)S(1)}, u32[]{:S(2)}, u32[]{:S(2)}) collective-permute-start(f32[8,384]{1,0:T(8,128)S(1)} %get-tuple-element.100), channel_id=1, source_target_pairs={{0,31},{1,0},{2,1},{3,2},{4,3},{5,4},{6,5},{7,6},{8,7},{9,8},{10,9... | collective-permute-start | bytes 36872 | tf_op jit(solution)/shard_map/ppermute | solution.py:379
  38.8 1.0 collective-permute-done.6.from_left
  39.8 1.6 %copy-done.1 = bf16[4096,256]{1,0:T(8,128)(2,1)S(1)} copy-done((bf16[4096,256]{1,0:T(8,128)(2,1)S(1)}, bf16[4096,256]{1,0:T(8,128)(2,1)}, u32[]{:S(2)}) %copy-start.1) | copy-done | bytes 2097176
  41.4 3.9 %shard_map.126 = (f32[96,128]{1,0:T(8,128)S(1)}, f32[8,2048]{1,0:T(8,128)S(1)}, f32[8,384]{1,0:T(8,128)S(1)}, f32[8,384]{1,0:T(8,128)S(1)}, f32[8,256]{1,0:T(8,128)S(1)}, /*index=5*/f32[8,256]{1,0:T(8,128)S(1)}) custom-call(s32[4]{0:T(128)S(1)} %add_convert_fusion.flags, f32[8,2048]{1,0:T(8,128)S(1)} %get-tuple-element.88.velocity, ...), custom_call_target="tpu_custom_call" | custom-call | tf_op jit(solution)/shard_map/pallas_call | solution.py:367
  45.3 0.9 collective-permute-start.8
  46.3 0.8 collective-permute-done.8.from_up
  47.1 3.5 %collective-permute-done.9.from_down = f32[8,384]{1,0:T(8,128)S(1)} collective-permute-done((f32[8,384]{1,0:T(8,128)S(1)}, f32[8,384]{1,0:T(8,128)S(1)}, u32[]{:S(2)}, u32[]{:S(2)}) %collective-permute-start.9) | collective-permute-done | bytes 12320 | tf_op jit(solution)/shard_map/ppermute | solution.py:379
  51.2 5.2 %collective-permute-start.11 = (f32[8,384]{1,0:T(8,128)S(1)}, f32[8,384]{1,0:T(8,128)S(1)}, u32[]{:S(2)}, u32[]{:S(2)}) collective-permute-start(f32[8,384]{1,0:T(8,128)S(1)} %get-tuple-element.107), channel_id=1, source_target_pairs={{0,31},{1,0},{2,1},{3,2},{4,3},{5,4},{6,5},{7,6},{8,7},{9,8},{10,9... | collective-permute-start | bytes 36872 | tf_op jit(solution)/shard_map/ppermute | solution.py:379
  56.5 1.0 collective-permute-done.10.from_left
  57.5 1.2 shard_map.128
  58.6 0.9 collective-permute-start.12
  60.4 3.5 %collective-permute-done.13.from_down = f32[8,384]{1,0:T(8,128)S(1)} collective-permute-done((f32[8,384]{1,0:T(8,128)S(1)}, f32[8,384]{1,0:T(8,128)S(1)}, u32[]{:S(2)}, u32[]{:S(2)}) %collective-permute-start.13) | collective-permute-done | bytes 12320 | tf_op jit(solution)/shard_map/ppermute | solution.py:379
  64.5 5.4 %collective-permute-start.15 = (f32[8,384]{1,0:T(8,128)S(1)}, f32[8,384]{1,0:T(8,128)S(1)}, u32[]{:S(2)}, u32[]{:S(2)}) collective-permute-start(f32[8,384]{1,0:T(8,128)S(1)} %get-tuple-element.115), channel_id=1, source_target_pairs={{0,31},{1,0},{2,1},{3,2},{4,3},{5,4},{6,5},{7,6},{8,7},{9,8},{10,9... | collective-permute-start | bytes 36872 | tf_op jit(solution)/shard_map/ppermute | solution.py:379
  70.8 4.0 %shard_map.130 = (f32[96,128]{1,0:T(8,128)S(1)}, f32[8,2048]{1,0:T(8,128)S(1)}, f32[8,384]{1,0:T(8,128)S(1)}, f32[8,384]{1,0:T(8,128)S(1)}, f32[8,256]{1,0:T(8,128)S(1)}, /*index=5*/f32[8,256]{1,0:T(8,128)S(1)}) custom-call(s32[4]{0:T(128)S(1)} %add_convert_fusion.flags, f32[8,2048]{1,0:T(8,128)S(1)} %get-tuple-element.108.velocity, ...), custom_call_target="tpu_custom_call" | custom-call | tf_op jit(solution)/shard_map/pallas_call | solution.py:367
  74.7 0.9 collective-permute-start.16
  76.5 3.5 %collective-permute-done.17.from_down = f32[8,384]{1,0:T(8,128)S(1)} collective-permute-done((f32[8,384]{1,0:T(8,128)S(1)}, f32[8,384]{1,0:T(8,128)S(1)}, u32[]{:S(2)}, u32[]{:S(2)}) %collective-permute-start.17) | collective-permute-done | bytes 12320 | tf_op jit(solution)/shard_map/ppermute | solution.py:379
  80.6 5.4 %collective-permute-start.19 = (f32[8,384]{1,0:T(8,128)S(1)}, f32[8,384]{1,0:T(8,128)S(1)}, u32[]{:S(2)}, u32[]{:S(2)}) collective-permute-start(f32[8,384]{1,0:T(8,128)S(1)} %get-tuple-element.122), channel_id=1, source_target_pairs={{0,31},{1,0},{2,1},{3,2},{4,3},{5,4},{6,5},{7,6},{8,7},{9,8},{10,9... | collective-permute-start | bytes 36872 | tf_op jit(solution)/shard_map/ppermute | solution.py:379
  86.0 1.0 collective-permute-done.18.from_left
  87.0 1.2 shard_map.132
  88.2 0.9 collective-permute-start.20
  90.0 3.5 %collective-permute-done.21.from_down = f32[8,384]{1,0:T(8,128)S(1)} collective-permute-done((f32[8,384]{1,0:T(8,128)S(1)}, f32[8,384]{1,0:T(8,128)S(1)}, u32[]{:S(2)}, u32[]{:S(2)}) %collective-permute-start.21) | collective-permute-done | bytes 12320 | tf_op jit(solution)/shard_map/ppermute | solution.py:379
  94.1 5.2 %collective-permute-start.23 = (f32[8,384]{1,0:T(8,128)S(1)}, f32[8,384]{1,0:T(8,128)S(1)}, u32[]{:S(2)}, u32[]{:S(2)}) collective-permute-start(f32[8,384]{1,0:T(8,128)S(1)} %get-tuple-element.130), channel_id=1, source_target_pairs={{0,31},{1,0},{2,1},{3,2},{4,3},{5,4},{6,5},{7,6},{8,7},{9,8},{10,9... | collective-permute-start | bytes 36872 | tf_op jit(solution)/shard_map/ppermute | solution.py:379
  99.3 1.0 collective-permute-done.22.from_left
  100.3 4.0 %shard_map.134 = (f32[96,128]{1,0:T(8,128)S(1)}, f32[8,2048]{1,0:T(8,128)S(1)}, f32[8,384]{1,0:T(8,128)S(1)}, f32[8,384]{1,0:T(8,128)S(1)}, f32[8,256]{1,0:T(8,128)S(1)}, /*index=5*/f32[8,256]{1,0:T(8,128)S(1)}) custom-call(s32[4]{0:T(128)S(1)} %add_convert_fusion.flags, f32[8,2048]{1,0:T(8,128)S(1)} %get-tuple-element.123.velocity, ...), custom_call_target="tpu_custom_call" | custom-call | tf_op jit(solution)/shard_map/pallas_call | solution.py:367
  104.3 0.9 collective-permute-start.24
  106.0 3.5 %collective-permute-done.25.from_down = f32[8,384]{1,0:T(8,128)S(1)} collective-permute-done((f32[8,384]{1,0:T(8,128)S(1)}, f32[8,384]{1,0:T(8,128)S(1)}, u32[]{:S(2)}, u32[]{:S(2)}) %collective-permute-start.25) | collective-permute-done | bytes 12320 | tf_op jit(solution)/shard_map/ppermute | solution.py:379
  110.2 5.2 %collective-permute-start.27 = (f32[8,384]{1,0:T(8,128)S(1)}, f32[8,384]{1,0:T(8,128)S(1)}, u32[]{:S(2)}, u32[]{:S(2)}) collective-permute-start(f32[8,384]{1,0:T(8,128)S(1)} %get-tuple-element.137), channel_id=1, source_target_pairs={{0,31},{1,0},{2,1},{3,2},{4,3},{5,4},{6,5},{7,6},{8,7},{9,8},{10,9... | collective-permute-start | bytes 36872 | tf_op jit(solution)/shard_map/ppermute | solution.py:379
  115.4 1.0 collective-permute-done.26.from_left
  116.4 1.2 shard_map.136
  117.6 0.9 collective-permute-start.28
  119.3 3.5 %collective-permute-done.29.from_down = f32[8,384]{1,0:T(8,128)S(1)} collective-permute-done((f32[8,384]{1,0:T(8,128)S(1)}, f32[8,384]{1,0:T(8,128)S(1)}, u32[]{:S(2)}, u32[]{:S(2)}) %collective-permute-start.29) | collective-permute-done | bytes 12320 | tf_op jit(solution)/shard_map/ppermute | solution.py:379
  123.5 5.4 %collective-permute-start.31 = (f32[8,384]{1,0:T(8,128)S(1)}, f32[8,384]{1,0:T(8,128)S(1)}, u32[]{:S(2)}, u32[]{:S(2)}) collective-permute-start(f32[8,384]{1,0:T(8,128)S(1)} %get-tuple-element.145), channel_id=1, source_target_pairs={{0,31},{1,0},{2,1},{3,2},{4,3},{5,4},{6,5},{7,6},{8,7},{9,8},{10,9... | collective-permute-start | bytes 36872 | tf_op jit(solution)/shard_map/ppermute | solution.py:379
  129.8 4.4 %shard_map.138 = (f32[96,128]{1,0:T(8,128)}, f32[8,2048]{1,0:T(8,128)S(1)}, f32[8,384]{1,0:T(8,128)S(1)}, f32[8,384]{1,0:T(8,128)S(1)}, f32[8,256]{1,0:T(8,128)S(1)}, /*index=5*/f32[8,256]{1,0:T(8,128)S(1)}) custom-call(s32[4]{0:T(128)S(1)} %add_convert_fusion.flags, f32[8,2048]{1,0:T(8,128)S(1)} %get-tuple-element.138.velocity, ...), custom_call_target="tpu_custom_call" | custom-call | tf_op jit(solution)/shard_map/pallas_call | solution.py:367
  134.1 0.9 collective-permute-start.32
  135.8 3.5 %collective-permute-done.33.from_down = f32[8,384]{1,0:T(8,128)S(1)} collective-permute-done((f32[8,384]{1,0:T(8,128)S(1)}, f32[8,384]{1,0:T(8,128)S(1)}, u32[]{:S(2)}, u32[]{:S(2)}) %collective-permute-start.33) | collective-permute-done | bytes 12320 | tf_op jit(solution)/shard_map/ppermute | solution.py:379
  140.0 5.4 %collective-permute-start.35 = (f32[8,384]{1,0:T(8,128)S(1)}, f32[8,384]{1,0:T(8,128)S(1)}, u32[]{:S(2)}, u32[]{:S(2)}) collective-permute-start(f32[8,384]{1,0:T(8,128)S(1)} %get-tuple-element.152), channel_id=1, source_target_pairs={{0,31},{1,0},{2,1},{3,2},{4,3},{5,4},{6,5},{7,6},{8,7},{9,8},{10,9... | collective-permute-start | bytes 36872 | tf_op jit(solution)/shard_map/ppermute | solution.py:379
  145.4 1.0 collective-permute-done.34.from_left
  146.4 0.8 shard_map.140
  (71 shorter events, 21.3 us)
Async XLA Ops:
  1.5 0.8 copy-start.3
  2.2 0.8 copy-start.4
  3.0 0.7 copy-start.5
  3.7 0.7 copy-start.6
  4.4 0.7 copy-start.7
  5.1 0.7 copy-start.8
  5.9 0.7 copy-start.9
  6.6 0.7 copy-start.10
  7.2 0.7 copy-start.11
  10.8 1.3 copy-start
  12.2 3.1 %collective-permute-start = (f32[8,384]{1,0:T(8,128)S(1)}, f32[8,384]{1,0:T(8,128)S(1)}, u32[]{:S(2)}, u32[]{:S(2)}) collective-permute-start(f32[8,384]{1,0:T(8,128)S(1)} %get-tuple-element.82), channel_id=1, source_target_pairs={{0,32},{32,64},{64,96},{96,128},{128,160},{160,192},{192,224},{224... | collective-permute-start | bytes 36872 | tf_op jit(solution)/shard_map/ppermute | solution.py:379
  14.4 4.3 %collective-permute-start.1 = (f32[8,384]{1,0:T(8,128)S(1)}, f32[8,384]{1,0:T(8,128)S(1)}, u32[]{:S(2)}, u32[]{:S(2)}) collective-permute-start(f32[8,384]{1,0:T(8,128)S(1)} %get-tuple-element.83), channel_id=1, source_target_pairs={{0,224},{32,0},{64,32},{96,64},{128,96},{160,128},{192,160},{224,1... | collective-permute-start | bytes 36872 | tf_op jit(solution)/shard_map/ppermute | solution.py:379
  19.3 7.2 %collective-permute-start.2 = (f32[8,384]{1,0:T(8,128)S(1)}, f32[8,384]{1,0:T(8,128)S(1)}, u32[]{:S(2)}, u32[]{:S(2)}) collective-permute-start(f32[8,384]{1,0:T(8,128)S(1)} %get-tuple-element.86), channel_id=1, source_target_pairs={{0,1},{1,2},{2,3},{3,4},{4,5},{5,6},{6,7},{7,8},{8,9},{9,10},{10,1... | collective-permute-start | bytes 36872 | tf_op jit(solution)/shard_map/ppermute | solution.py:379
  19.4 7.1 %collective-permute-start.3 = (f32[8,384]{1,0:T(8,128)S(1)}, f32[8,384]{1,0:T(8,128)S(1)}, u32[]{:S(2)}, u32[]{:S(2)}) collective-permute-start(f32[8,384]{1,0:T(8,128)S(1)} %get-tuple-element.87), channel_id=1, source_target_pairs={{0,31},{1,0},{2,1},{3,2},{4,3},{5,4},{6,5},{7,6},{8,7},{9,8},{10,9... | collective-permute-start | bytes 36872 | tf_op jit(solution)/shard_map/ppermute | solution.py:379
  27.7 1.7 %collective-permute-start.4 = (f32[8,384]{1,0:T(8,128)S(1)}, f32[8,384]{1,0:T(8,128)S(1)}, u32[]{:S(2)}, u32[]{:S(2)}) collective-permute-start(f32[8,384]{1,0:T(8,128)S(1)} %get-tuple-element.95), channel_id=1, source_target_pairs={{0,32},{32,64},{64,96},{96,128},{128,160},{160,192},{192,224},{224... | collective-permute-start | bytes 36872 | tf_op jit(solution)/shard_map/ppermute | solution.py:379
  28.6 4.3 %collective-permute-start.5 = (f32[8,384]{1,0:T(8,128)S(1)}, f32[8,384]{1,0:T(8,128)S(1)}, u32[]{:S(2)}, u32[]{:S(2)}) collective-permute-start(f32[8,384]{1,0:T(8,128)S(1)} %get-tuple-element.96), channel_id=1, source_target_pairs={{0,224},{32,0},{64,32},{96,64},{128,96},{160,128},{192,160},{224,1... | collective-permute-start | bytes 36872 | tf_op jit(solution)/shard_map/ppermute | solution.py:379
  33.5 6.3 %collective-permute-start.6 = (f32[8,384]{1,0:T(8,128)S(1)}, f32[8,384]{1,0:T(8,128)S(1)}, u32[]{:S(2)}, u32[]{:S(2)}) collective-permute-start(f32[8,384]{1,0:T(8,128)S(1)} %get-tuple-element.99), channel_id=1, source_target_pairs={{0,1},{1,2},{2,3},{3,4},{4,5},{5,6},{6,7},{7,8},{8,9},{9,10},{10,1... | collective-permute-start | bytes 36872 | tf_op jit(solution)/shard_map/ppermute | solution.py:379
  33.6 6.2 %collective-permute-start.7 = (f32[8,384]{1,0:T(8,128)S(1)}, f32[8,384]{1,0:T(8,128)S(1)}, u32[]{:S(2)}, u32[]{:S(2)}) collective-permute-start(f32[8,384]{1,0:T(8,128)S(1)} %get-tuple-element.100), channel_id=1, source_target_pairs={{0,31},{1,0},{2,1},{3,2},{4,3},{5,4},{6,5},{7,6},{8,7},{9,8},{10,9... | collective-permute-start | bytes 36872 | tf_op jit(solution)/shard_map/ppermute | solution.py:379
  39.8 1.6 %copy-start.1 = (bf16[4096,256]{1,0:T(8,128)(2,1)S(1)}, bf16[4096,256]{1,0:T(8,128)(2,1)}, u32[]{:S(2)}) copy-start(bf16[4096,256]{1,0:T(8,128)(2,1)} %copy-done) | copy-start | bytes 6291460
  41.4 29.4 %copy-start.2 = (bf16[4096,256]{1,0:T(8,128)(2,1)S(1)}, bf16[4096,256]{1,0:T(8,128)(2,1)}, u32[]{:S(2)}) copy-start(bf16[4096,256]{1,0:T(8,128)(2,1)} %copy-done) | copy-start | bytes 6291460
  45.3 1.7 %collective-permute-start.8 = (f32[8,384]{1,0:T(8,128)S(1)}, f32[8,384]{1,0:T(8,128)S(1)}, u32[]{:S(2)}, u32[]{:S(2)}) collective-permute-start(f32[8,384]{1,0:T(8,128)S(1)} %get-tuple-element.102), channel_id=1, source_target_pairs={{0,32},{32,64},{64,96},{96,128},{128,160},{160,192},{192,224},{224... | collective-permute-start | bytes 36872 | tf_op jit(solution)/shard_map/ppermute | solution.py:379
  46.3 4.3 %collective-permute-start.9 = (f32[8,384]{1,0:T(8,128)S(1)}, f32[8,384]{1,0:T(8,128)S(1)}, u32[]{:S(2)}, u32[]{:S(2)}) collective-permute-start(f32[8,384]{1,0:T(8,128)S(1)} %get-tuple-element.103), channel_id=1, source_target_pairs={{0,224},{32,0},{64,32},{96,64},{128,96},{160,128},{192,160},{224,1... | collective-permute-start | bytes 36872 | tf_op jit(solution)/shard_map/ppermute | solution.py:379
  51.1 6.3 %collective-permute-start.10 = (f32[8,384]{1,0:T(8,128)S(1)}, f32[8,384]{1,0:T(8,128)S(1)}, u32[]{:S(2)}, u32[]{:S(2)}) collective-permute-start(f32[8,384]{1,0:T(8,128)S(1)} %get-tuple-element.106), channel_id=1, source_target_pairs={{0,1},{1,2},{2,3},{3,4},{4,5},{5,6},{6,7},{7,8},{8,9},{9,10},{10,1... | collective-permute-start | bytes 36872 | tf_op jit(solution)/shard_map/ppermute | solution.py:379
  51.2 6.2 %collective-permute-start.11 = (f32[8,384]{1,0:T(8,128)S(1)}, f32[8,384]{1,0:T(8,128)S(1)}, u32[]{:S(2)}, u32[]{:S(2)}) collective-permute-start(f32[8,384]{1,0:T(8,128)S(1)} %get-tuple-element.107), channel_id=1, source_target_pairs={{0,31},{1,0},{2,1},{3,2},{4,3},{5,4},{6,5},{7,6},{8,7},{9,8},{10,9... | collective-permute-start | bytes 36872 | tf_op jit(solution)/shard_map/ppermute | solution.py:379
  58.6 1.7 %collective-permute-start.12 = (f32[8,384]{1,0:T(8,128)S(1)}, f32[8,384]{1,0:T(8,128)S(1)}, u32[]{:S(2)}, u32[]{:S(2)}) collective-permute-start(f32[8,384]{1,0:T(8,128)S(1)} %get-tuple-element.110), channel_id=1, source_target_pairs={{0,32},{32,64},{64,96},{96,128},{128,160},{160,192},{192,224},{224... | collective-permute-start | bytes 36872 | tf_op jit(solution)/shard_map/ppermute | solution.py:379
  59.6 4.3 %collective-permute-start.13 = (f32[8,384]{1,0:T(8,128)S(1)}, f32[8,384]{1,0:T(8,128)S(1)}, u32[]{:S(2)}, u32[]{:S(2)}) collective-permute-start(f32[8,384]{1,0:T(8,128)S(1)} %get-tuple-element.111), channel_id=1, source_target_pairs={{0,224},{32,0},{64,32},{96,64},{128,96},{160,128},{192,160},{224,1... | collective-permute-start | bytes 36872 | tf_op jit(solution)/shard_map/ppermute | solution.py:379
  64.4 6.3 %collective-permute-start.14 = (f32[8,384]{1,0:T(8,128)S(1)}, f32[8,384]{1,0:T(8,128)S(1)}, u32[]{:S(2)}, u32[]{:S(2)}) collective-permute-start(f32[8,384]{1,0:T(8,128)S(1)} %get-tuple-element.114), channel_id=1, source_target_pairs={{0,1},{1,2},{2,3},{3,4},{4,5},{5,6},{6,7},{7,8},{8,9},{9,10},{10,1... | collective-permute-start | bytes 36872 | tf_op jit(solution)/shard_map/ppermute | solution.py:379
  64.5 6.2 %collective-permute-start.15 = (f32[8,384]{1,0:T(8,128)S(1)}, f32[8,384]{1,0:T(8,128)S(1)}, u32[]{:S(2)}, u32[]{:S(2)}) collective-permute-start(f32[8,384]{1,0:T(8,128)S(1)} %get-tuple-element.115), channel_id=1, source_target_pairs={{0,31},{1,0},{2,1},{3,2},{4,3},{5,4},{6,5},{7,6},{8,7},{9,8},{10,9... | collective-permute-start | bytes 36872 | tf_op jit(solution)/shard_map/ppermute | solution.py:379
  74.7 1.7 %collective-permute-start.16 = (f32[8,384]{1,0:T(8,128)S(1)}, f32[8,384]{1,0:T(8,128)S(1)}, u32[]{:S(2)}, u32[]{:S(2)}) collective-permute-start(f32[8,384]{1,0:T(8,128)S(1)} %get-tuple-element.117), channel_id=1, source_target_pairs={{0,32},{32,64},{64,96},{96,128},{128,160},{160,192},{192,224},{224... | collective-permute-start | bytes 36872 | tf_op jit(solution)/shard_map/ppermute | solution.py:379
  75.6 4.3 %collective-permute-start.17 = (f32[8,384]{1,0:T(8,128)S(1)}, f32[8,384]{1,0:T(8,128)S(1)}, u32[]{:S(2)}, u32[]{:S(2)}) collective-permute-start(f32[8,384]{1,0:T(8,128)S(1)} %get-tuple-element.118), channel_id=1, source_target_pairs={{0,224},{32,0},{64,32},{96,64},{128,96},{160,128},{192,160},{224,1... | collective-permute-start | bytes 36872 | tf_op jit(solution)/shard_map/ppermute | solution.py:379
  80.5 6.5 %collective-permute-start.18 = (f32[8,384]{1,0:T(8,128)S(1)}, f32[8,384]{1,0:T(8,128)S(1)}, u32[]{:S(2)}, u32[]{:S(2)}) collective-permute-start(f32[8,384]{1,0:T(8,128)S(1)} %get-tuple-element.121), channel_id=1, source_target_pairs={{0,1},{1,2},{2,3},{3,4},{4,5},{5,6},{6,7},{7,8},{8,9},{9,10},{10,1... | collective-permute-start | bytes 36872 | tf_op jit(solution)/shard_map/ppermute | solution.py:379
  80.6 6.4 %collective-permute-start.19 = (f32[8,384]{1,0:T(8,128)S(1)}, f32[8,384]{1,0:T(8,128)S(1)}, u32[]{:S(2)}, u32[]{:S(2)}) collective-permute-start(f32[8,384]{1,0:T(8,128)S(1)} %get-tuple-element.122), channel_id=1, source_target_pairs={{0,31},{1,0},{2,1},{3,2},{4,3},{5,4},{6,5},{7,6},{8,7},{9,8},{10,9... | collective-permute-start | bytes 36872 | tf_op jit(solution)/shard_map/ppermute | solution.py:379
  88.2 1.7 %collective-permute-start.20 = (f32[8,384]{1,0:T(8,128)S(1)}, f32[8,384]{1,0:T(8,128)S(1)}, u32[]{:S(2)}, u32[]{:S(2)}) collective-permute-start(f32[8,384]{1,0:T(8,128)S(1)} %get-tuple-element.125), channel_id=1, source_target_pairs={{0,32},{32,64},{64,96},{96,128},{128,160},{160,192},{192,224},{224... | collective-permute-start | bytes 36872 | tf_op jit(solution)/shard_map/ppermute | solution.py:379
  89.1 4.3 %collective-permute-start.21 = (f32[8,384]{1,0:T(8,128)S(1)}, f32[8,384]{1,0:T(8,128)S(1)}, u32[]{:S(2)}, u32[]{:S(2)}) collective-permute-start(f32[8,384]{1,0:T(8,128)S(1)} %get-tuple-element.126), channel_id=1, source_target_pairs={{0,224},{32,0},{64,32},{96,64},{128,96},{160,128},{192,160},{224,1... | collective-permute-start | bytes 36872 | tf_op jit(solution)/shard_map/ppermute | solution.py:379
  94.0 6.3 %collective-permute-start.22 = (f32[8,384]{1,0:T(8,128)S(1)}, f32[8,384]{1,0:T(8,128)S(1)}, u32[]{:S(2)}, u32[]{:S(2)}) collective-permute-start(f32[8,384]{1,0:T(8,128)S(1)} %get-tuple-element.129), channel_id=1, source_target_pairs={{0,1},{1,2},{2,3},{3,4},{4,5},{5,6},{6,7},{7,8},{8,9},{9,10},{10,1... | collective-permute-start | bytes 36872 | tf_op jit(solution)/shard_map/ppermute | solution.py:379
  94.1 6.2 %collective-permute-start.23 = (f32[8,384]{1,0:T(8,128)S(1)}, f32[8,384]{1,0:T(8,128)S(1)}, u32[]{:S(2)}, u32[]{:S(2)}) collective-permute-start(f32[8,384]{1,0:T(8,128)S(1)} %get-tuple-element.130), channel_id=1, source_target_pairs={{0,31},{1,0},{2,1},{3,2},{4,3},{5,4},{6,5},{7,6},{8,7},{9,8},{10,9... | collective-permute-start | bytes 36872 | tf_op jit(solution)/shard_map/ppermute | solution.py:379
  104.3 1.7 %collective-permute-start.24 = (f32[8,384]{1,0:T(8,128)S(1)}, f32[8,384]{1,0:T(8,128)S(1)}, u32[]{:S(2)}, u32[]{:S(2)}) collective-permute-start(f32[8,384]{1,0:T(8,128)S(1)} %get-tuple-element.132), channel_id=1, source_target_pairs={{0,32},{32,64},{64,96},{96,128},{128,160},{160,192},{192,224},{224... | collective-permute-start | bytes 36872 | tf_op jit(solution)/shard_map/ppermute | solution.py:379
  105.2 4.3 %collective-permute-start.25 = (f32[8,384]{1,0:T(8,128)S(1)}, f32[8,384]{1,0:T(8,128)S(1)}, u32[]{:S(2)}, u32[]{:S(2)}) collective-permute-start(f32[8,384]{1,0:T(8,128)S(1)} %get-tuple-element.133), channel_id=1, source_target_pairs={{0,224},{32,0},{64,32},{96,64},{128,96},{160,128},{192,160},{224,1... | collective-permute-start | bytes 36872 | tf_op jit(solution)/shard_map/ppermute | solution.py:379
  110.1 6.3 %collective-permute-start.26 = (f32[8,384]{1,0:T(8,128)S(1)}, f32[8,384]{1,0:T(8,128)S(1)}, u32[]{:S(2)}, u32[]{:S(2)}) collective-permute-start(f32[8,384]{1,0:T(8,128)S(1)} %get-tuple-element.136), channel_id=1, source_target_pairs={{0,1},{1,2},{2,3},{3,4},{4,5},{5,6},{6,7},{7,8},{8,9},{9,10},{10,1... | collective-permute-start | bytes 36872 | tf_op jit(solution)/shard_map/ppermute | solution.py:379
  110.2 6.2 %collective-permute-start.27 = (f32[8,384]{1,0:T(8,128)S(1)}, f32[8,384]{1,0:T(8,128)S(1)}, u32[]{:S(2)}, u32[]{:S(2)}) collective-permute-start(f32[8,384]{1,0:T(8,128)S(1)} %get-tuple-element.137), channel_id=1, source_target_pairs={{0,31},{1,0},{2,1},{3,2},{4,3},{5,4},{6,5},{7,6},{8,7},{9,8},{10,9... | collective-permute-start | bytes 36872 | tf_op jit(solution)/shard_map/ppermute | solution.py:379
  117.6 1.7 %collective-permute-start.28 = (f32[8,384]{1,0:T(8,128)S(1)}, f32[8,384]{1,0:T(8,128)S(1)}, u32[]{:S(2)}, u32[]{:S(2)}) collective-permute-start(f32[8,384]{1,0:T(8,128)S(1)} %get-tuple-element.140), channel_id=1, source_target_pairs={{0,32},{32,64},{64,96},{96,128},{128,160},{160,192},{192,224},{224... | collective-permute-start | bytes 36872 | tf_op jit(solution)/shard_map/ppermute | solution.py:379
  118.5 4.3 %collective-permute-start.29 = (f32[8,384]{1,0:T(8,128)S(1)}, f32[8,384]{1,0:T(8,128)S(1)}, u32[]{:S(2)}, u32[]{:S(2)}) collective-permute-start(f32[8,384]{1,0:T(8,128)S(1)} %get-tuple-element.141), channel_id=1, source_target_pairs={{0,224},{32,0},{64,32},{96,64},{128,96},{160,128},{192,160},{224,1... | collective-permute-start | bytes 36872 | tf_op jit(solution)/shard_map/ppermute | solution.py:379
  123.4 6.3 %collective-permute-start.30 = (f32[8,384]{1,0:T(8,128)S(1)}, f32[8,384]{1,0:T(8,128)S(1)}, u32[]{:S(2)}, u32[]{:S(2)}) collective-permute-start(f32[8,384]{1,0:T(8,128)S(1)} %get-tuple-element.144), channel_id=1, source_target_pairs={{0,1},{1,2},{2,3},{3,4},{4,5},{5,6},{6,7},{7,8},{8,9},{9,10},{10,1... | collective-permute-start | bytes 36872 | tf_op jit(solution)/shard_map/ppermute | solution.py:379
  123.5 6.3 %collective-permute-start.31 = (f32[8,384]{1,0:T(8,128)S(1)}, f32[8,384]{1,0:T(8,128)S(1)}, u32[]{:S(2)}, u32[]{:S(2)}) collective-permute-start(f32[8,384]{1,0:T(8,128)S(1)} %get-tuple-element.145), channel_id=1, source_target_pairs={{0,31},{1,0},{2,1},{3,2},{4,3},{5,4},{6,5},{7,6},{8,7},{9,8},{10,9... | collective-permute-start | bytes 36872 | tf_op jit(solution)/shard_map/ppermute | solution.py:379
  134.1 1.7 %collective-permute-start.32 = (f32[8,384]{1,0:T(8,128)S(1)}, f32[8,384]{1,0:T(8,128)S(1)}, u32[]{:S(2)}, u32[]{:S(2)}) collective-permute-start(f32[8,384]{1,0:T(8,128)S(1)} %get-tuple-element.147), channel_id=1, source_target_pairs={{0,32},{32,64},{64,96},{96,128},{128,160},{160,192},{192,224},{224... | collective-permute-start | bytes 36872 | tf_op jit(solution)/shard_map/ppermute | solution.py:379
  135.0 4.3 %collective-permute-start.33 = (f32[8,384]{1,0:T(8,128)S(1)}, f32[8,384]{1,0:T(8,128)S(1)}, u32[]{:S(2)}, u32[]{:S(2)}) collective-permute-start(f32[8,384]{1,0:T(8,128)S(1)} %get-tuple-element.148), channel_id=1, source_target_pairs={{0,224},{32,0},{64,32},{96,64},{128,96},{160,128},{192,160},{224,1... | collective-permute-start | bytes 36872 | tf_op jit(solution)/shard_map/ppermute | solution.py:379
  139.9 6.5 %collective-permute-start.34 = (f32[8,384]{1,0:T(8,128)S(1)}, f32[8,384]{1,0:T(8,128)S(1)}, u32[]{:S(2)}, u32[]{:S(2)}) collective-permute-start(f32[8,384]{1,0:T(8,128)S(1)} %get-tuple-element.151), channel_id=1, source_target_pairs={{0,1},{1,2},{2,3},{3,4},{4,5},{5,6},{6,7},{7,8},{8,9},{9,10},{10,1... | collective-permute-start | bytes 36872 | tf_op jit(solution)/shard_map/ppermute | solution.py:379
  140.0 6.4 %collective-permute-start.35 = (f32[8,384]{1,0:T(8,128)S(1)}, f32[8,384]{1,0:T(8,128)S(1)}, u32[]{:S(2)}, u32[]{:S(2)}) collective-permute-start(f32[8,384]{1,0:T(8,128)S(1)} %get-tuple-element.152), channel_id=1, source_target_pairs={{0,31},{1,0},{2,1},{3,2},{4,3},{5,4},{6,5},{7,6},{8,7},{9,8},{10,9... | collective-permute-start | bytes 36872 | tf_op jit(solution)/shard_map/ppermute | solution.py:379

commit v2 on v1

v2 whole, which is shorter than its diff:
```python
import jax
import jax.numpy as jnp
from jax import lax
from jax.experimental import pallas as pl
from jax.experimental.pallas import tpu as pltpu
from jax.sharding import PartitionSpec as P

SWEEPS = 4
RELAX = 0.25
SMALLEST = 1e-20

BODY = 2048
FACE = 256
CORNER = 32
CONTACTS = 4096
ROWS = CONTACTS // 128
LISTED = 4 * FACE + 4 * CORNER
LIST_ROWS = LISTED // 128
OWN_TILES = BODY // 128
WIDE = 256
OWN_WIDE = BODY // WIDE
GHOST_WIDE = 6
IMPULSE_ROWS = 3 * ROWS
MESSAGE = FACE + 128

F32 = jnp.float32
BF16 = jnp.bfloat16
I32 = jnp.int32

PLANES = (
    "n0", "n1", "n2", "a0", "a1", "b0", "b1", "b2",
    "arm0", "arm1", "relax", "mu", "bias",
)
PLANE = {name: place for place, name in enumerate(PLANES)}


def lanes_of(table, lane):
    numbers = lax.GatherDimensionNumbers(
        offset_dims=(),
        collapsed_slice_dims=(1,),
        start_index_map=(1,),
        operand_batching_dims=(0,),
        start_indices_batching_dims=(0,),
    )
    return lax.gather(
        table, lane[..., None], numbers, (1, 1),
        mode=lax.GatherScatterMode.PROMISE_IN_BOUNDS,
    )


def iota(shape, dim):
    return lax.broadcasted_iota(I32, shape, dim)


def halves(values):
    high = values.astype(BF16).astype(F32)
    return high, values - high


def plane(ref, number):
    return ref[number * ROWS:(number + 1) * ROWS, :]


def spread(ref, high_row, parts, blocks, column):
    picks = [high_row == block for block in blocks]
    for part, value in enumerate(parts):
        zero = jnp.zeros_like(value)
        for pair in range(len(blocks) // 2):
            both = jnp.concatenate(
                [
                    jnp.where(picks[2 * pair], value, zero),
                    jnp.where(picks[2 * pair + 1], value, zero),
                ],
                axis=0,
            )
            start = part * len(blocks) * 8 + pair * 16
            ref[start:start + 16, column:column + 128] = both.astype(BF16)


OWN_BLOCKS = tuple(range(OWN_WIDE))
GHOST_BLOCKS = tuple(range(OWN_WIDE, OWN_WIDE + GHOST_WIDE))


def lane_hot(ref, low, rows):
    turned = jnp.transpose(low)
    along = iota((128, WIDE), 1)
    for row in range(rows):
        hot = jnp.broadcast_to(turned[:, row:row + 1], (128, WIDE)) == along
        ref[row * 128:(row + 1) * 128, :] = jnp.where(hot, 1.0, 0.0).astype(BF16)


def product(left, hot, blocks):
    total = jnp.dot(left[...], hot, preferred_element_type=F32)
    return total[:blocks * 8] + total[blocks * 8:]


def end_pulses(impulse, table, near_out, far_out):
    p0, p1, p2 = impulse
    get = lambda name: plane(table, PLANE[name])
    a0, a1 = get("a0"), get("a1")
    b0, b1, b2 = get("b0"), get("b1"), get("b2")
    force = (
        p0 * get("n0") + p1 * a0 + p2 * b0,
        p0 * get("n1") + p1 * a1 + p2 * b1,
        p0 * get("n2") + p2 * b2,
    )
    twist = (p1 * b0 - p2 * a0, p1 * b1 - p2 * a1, p1 * b2)
    arm0, arm1 = -get("arm0"), -get("arm1")
    for comp in range(3):
        near_out[pl.ds(comp, ROWS, stride=8), :] = force[comp]
        far_out[pl.ds(comp, ROWS, stride=8), :] = -force[comp]
        near_out[pl.ds(comp + 3, ROWS, stride=8), :] = arm0 * twist[comp]
        far_out[pl.ds(comp + 3, ROWS, stride=8), :] = arm1 * twist[comp]
    for comp in (6, 7):
        near_out[pl.ds(comp, ROWS, stride=8), :] = jnp.zeros((ROWS, 128), F32)
        far_out[pl.ds(comp, ROWS, stride=8), :] = jnp.zeros((ROWS, 128), F32)


def spread_rows(left, values, high, blocks):
    for row in range(ROWS):
        value = values[row * 8:(row + 1) * 8, :]
        spread(left, high[row:row + 1, :], halves(value), blocks, row * 128)


def ghost_pulses(far, high_far, hot_far, up, down, left, right, left_ghost):
    spread_rows(left_ghost, far, high_far, GHOST_BLOCKS)
    total = product(left_ghost, hot_far[...], GHOST_WIDE)
    ghost = [total[block * 8:block * 8 + 8] for block in range(5)]
    send_gx(ghost[0], ghost[1], ghost[4][:, :128], up, down)
    left[...] = ghost[2]
    right[...] = ghost[3]


def send_gx(face0, face1, corners, up, down):
    slot = iota((8, 128), 1) // CORNER
    to_down = (slot == 0) | (slot == 2)
    up[:, :FACE] = face0
    up[:, FACE:] = jnp.where(to_down, 0.0, corners)
    down[:, :FACE] = face1
    down[:, FACE:] = jnp.where(to_down, corners, 0.0)


def prepare(
    angles_in, arms_in, mu_in, bias_in, impulse_in, owner_in, other_in,
    radius_in, faces_in, corners_in, base_in,
    table, places, high_far, impulse, hot_far, near_values, far_values,
    up, down, left, right,
    owner, radius, faces, corners, base,
    angles, arms, mu, bias, other, flat, left_ghost, sems,
):
    copies = [
        pltpu.make_async_copy(source, target, sems.at[number])
        for number, (source, target) in enumerate((
            (other_in, other), (angles_in, angles), (arms_in, arms), (mu_in, mu),
            (bias_in, bias), (impulse_in, impulse), (owner_in, owner), (radius_in, radius),
            (faces_in, faces), (corners_in, corners), (base_in, base),
        ))
    ]
    for copy in copies:
        copy.start()
    copies[0].wait()
    far_id = other[...]
    extra = far_id - (BODY + 4 * FACE)
    block = extra >> 5
    slot = ((block & 1) << 1) | (block >> 1)
    in_block = extra & (CORNER - 1)
    is_corner = extra >= 0
    places[2 * ROWS:3 * ROWS, :] = far_id >> 7
    places[3 * ROWS:, :] = jnp.where(is_corner, slot * CORNER + in_block, far_id & 127)
    high_far[...] = far_id >> 8
    lane_hot(
        hot_far, jnp.where(is_corner, (3 - slot) * CORNER + in_block, far_id & 255), ROWS
    )
    for copy in copies[1:]:
        copy.wait()
    near_id = owner[...]
    places[:ROWS, :] = near_id >> 7
    places[ROWS:2 * ROWS, :] = near_id & 127
    for row in range(ROWS):
        cut = slice(row * 128, (row + 1) * 128)
        flat[pl.ds(row, 2, stride=ROWS), :] = angles[:, cut]
        flat[pl.ds(2 * ROWS + row, 2, stride=ROWS), :] = arms[:, cut]
    polar, azim = plane(flat, 0), plane(flat, 1)
    arm0, arm1 = plane(flat, 2), plane(flat, 3)
    cos_polar, sin_polar = jnp.cos(polar), jnp.sin(polar)
    cos_azim, sin_azim = jnp.cos(azim), jnp.sin(azim)
    cubed0 = arm0 * arm0 * arm0
    cubed1 = arm1 * arm1 * arm1
    values = {
        "n0": cos_polar * cos_azim, "n1": cos_polar * sin_azim, "n2": sin_polar,
        "a0": -sin_azim, "a1": cos_azim,
        "b0": -sin_polar * cos_azim, "b1": -sin_polar * sin_azim, "b2": cos_polar,
        "arm0": arm0, "arm1": arm1,
        "relax": RELAX / (1.0 / cubed0 + 1.0 / cubed1),
        "mu": mu[...], "bias": bias[...],
    }
    for name, value in values.items():
        number = PLANE[name]
        table[number * ROWS:(number + 1) * ROWS, :] = value
    end_pulses([plane(impulse, comp) for comp in range(3)], table, near_values, far_values)
    ghost_pulses(far_values, high_far, hot_far, up, down, left, right, left_ghost)


def prepare_own(
    near_values, owner, radius, faces, corners, base_rows,
    pulse, high_near, hot_near, hot_list, list_places, inverse, base,
    left_near,
):
    near_id = owner[...]
    high_near[...] = near_id >> 8
    lane_hot(hot_near, near_id & 255, ROWS)
    for number in range(4):
        for part in range(2):
            row = number * 2 + part
            list_places[row:row + 1, :] = faces[number:number + 1, part * 128:(part + 1) * 128]
    for place, number in enumerate((0, 2, 1, 3)):
        list_places[8:9, place * CORNER:(place + 1) * CORNER] = corners[number:number + 1, :]
    for place, number in enumerate((3, 1, 2, 0)):
        list_places[9:10, place * CORNER:(place + 1) * CORNER] = corners[number:number + 1, :]
    list_places[10:, :] = jnp.zeros((6, 128), I32)
    lane_hot(hot_list, list_places[...] & 255, LIST_ROWS)

    size = radius[...]
    cubed = size * size * size
    linear = 1.0 / cubed
    angular = 2.5 / (cubed * size * size)
    inverse[...] = jnp.where(iota((8, BODY), 0) < 3, linear, angular)
    for tile in range(OWN_TILES):
        base[:, tile * 128:(tile + 1) * 128] = base_rows[pl.ds(tile, 6, stride=OWN_TILES), :]
    scatter_near(near_values, high_near, hot_near, pulse, left_near)


def store_blocks(pulse, total):
    for block in range(OWN_WIDE):
        pulse[:, block * WIDE:(block + 1) * WIDE] = total[block * 8:block * 8 + 8]


def scatter_near(values, high_near, hot_near, pulse, left_near):
    spread_rows(left_near, values, high_near, OWN_BLOCKS)
    store_blocks(pulse, product(left_near, hot_near[...], OWN_WIDE))


def masked(flags, number, value):
    return jnp.where(flags[number:number + 1, :] > 0, value, jnp.zeros_like(value))


def gx_tiles(flags, from_up, from_down):
    return [
        masked(flags, number, ref[:, part * 128:(part + 1) * 128])
        for number, ref in enumerate((from_up, from_down))
        for part in range(2)
    ]


def gy_tiles(flags, from_left, from_right):
    tiles = [
        masked(flags, number + 2, ref[:, part * 128:(part + 1) * 128])
        for number, ref in enumerate((from_left, from_right))
        for part in range(2)
    ]
    early = iota((8, 128), 1) < 2 * CORNER
    corners = jnp.where(early, from_left[:, FACE:], from_right[:, FACE:])
    return tiles + [masked(flags, 4, corners)]


def list_product(left_list, tiles, list_places, hot, first):
    for row, tile in enumerate(tiles):
        high_row = list_places[first + row:first + row + 1, :] >> 8
        spread(left_list, high_row, halves(tile), OWN_BLOCKS, row * 128)
    rows = slice(first * 128, (first + len(tiles)) * 128)
    return product(left_list, hot[rows, :], OWN_WIDE)


def scatter_far(
    flags, values, high_far, hot_far, near_pulse, list_places, hot_list, from_up, from_down,
    pulse, left_far, left_list,
):
    spread_rows(left_far, values, high_far, OWN_BLOCKS)
    total = product(left_far, hot_far[...], OWN_WIDE)
    total = total + list_product(
        left_list, gx_tiles(flags, from_up, from_down), list_places, hot_list, 0
    )
    for block in range(OWN_WIDE):
        cut = slice(block * WIDE, (block + 1) * WIDE)
        pulse[:, cut] = near_pulse[:, cut] + total[block * 8:block * 8 + 8]


def settled(flags, own, inverse, base, list_places, hot_list, from_left, from_right, left_list):
    added = list_product(
        left_list, gy_tiles(flags, from_left, from_right), list_places, hot_list, 4
    )
    blocks = []
    for block in range(OWN_WIDE):
        cut = slice(block * WIDE, (block + 1) * WIDE)
        total = own[:6, cut] + added[block * 8:block * 8 + 6]
        blocks.append(base[:, cut] + inverse[:6, cut] * total)
    return blocks


def listed(velocity, list_places, row):
    entry = jnp.broadcast_to(list_places[row:row + 1, :], (8, 128))
    tile_id, lane = entry >> 7, entry & 127
    total = jnp.zeros((8, 128), F32)
    for tile in range(OWN_TILES):
        table = velocity[:, tile * 128:(tile + 1) * 128]
        total = jnp.where(tile_id == tile, lanes_of(table, lane), total)
    return total


def settle(
    flags, own, inverse, base, list_places, hot_list, from_left, from_right,
    velocity, up, down, left_list,
):
    blocks = settled(
        flags, own, inverse, base, list_places, hot_list, from_left, from_right, left_list
    )
    zero = jnp.zeros((2, WIDE), F32)
    for block, value in enumerate(blocks):
        velocity[:, block * WIDE:(block + 1) * WIDE] = jnp.concatenate([value, zero], axis=0)
    found = [listed(velocity, list_places, row) for row in (0, 1, 2, 3, 9)]
    face = [jnp.concatenate(found[2 * k:2 * k + 2], axis=1) for k in range(2)]
    send_gx(*face, found[4], up, down)


def settle_last(
    flags, own, inverse, base, list_places, hot_list, from_left, from_right,
    velocity, left_list,
):
    blocks = settled(
        flags, own, inverse, base, list_places, hot_list, from_left, from_right, left_list
    )
    for block, value in enumerate(blocks):
        for part in range(2):
            tile = 2 * block + part
            velocity[pl.ds(tile, 6, stride=OWN_TILES), :] = value[:, part * 128:(part + 1) * 128]


def pick(tables, tile_id, lane, firsts, totals):
    for tile, table in zip(firsts, tables):
        here = tile_id == tile
        for comp in range(6):
            row = jnp.broadcast_to(table[comp:comp + 1, :], (ROWS, 128))
            totals[comp] = jnp.where(here, lanes_of(row, lane), totals[comp])
    return totals


def own_tables(velocity):
    return [velocity[:, tile * 128:(tile + 1) * 128] for tile in range(OWN_TILES)]


def blank():
    return [jnp.zeros((ROWS, 128), F32) for _ in range(6)]


def gather_near(velocity, places, list_places, near, left, right):
    for row, (ref, part) in enumerate(((left, 0), (left, 1), (right, 0), (right, 1))):
        ref[:, part * 128:(part + 1) * 128] = listed(velocity, list_places, 4 + row)
    found = pick(
        own_tables(velocity), places[:ROWS, :], places[ROWS:2 * ROWS, :], range(OWN_TILES), blank()
    )
    for comp in range(6):
        near[comp * ROWS:(comp + 1) * ROWS, :] = found[comp]


def gather_far(flags, velocity, places, from_up, from_down, far):
    found = pick(
        own_tables(velocity) + gx_tiles(flags, from_up, from_down),
        places[2 * ROWS:3 * ROWS, :], places[3 * ROWS:, :], range(OWN_TILES + 4), blank(),
    )
    for comp in range(6):
        far[comp * ROWS:(comp + 1) * ROWS, :] = found[comp]


def sweep(
    flags, near_ref, far_ref, table, places, high_far, hot_far, impulse, from_left, from_right,
    impulse_out, near_values, far_values, up, down, left, right, left_ghost,
):
    near = [plane(near_ref, comp) for comp in range(6)]
    far = pick(
        gy_tiles(flags, from_left, from_right),
        places[2 * ROWS:3 * ROWS, :], places[3 * ROWS:, :],
        range(OWN_TILES + 4, OWN_TILES + 9), [plane(far_ref, comp) for comp in range(6)],
    )
    get = lambda name: plane(table, PLANE[name])
    n0, n1, n2 = get("n0"), get("n1"), get("n2")
    a0, a1 = get("a0"), get("a1")
    b0, b1, b2 = get("b0"), get("b1"), get("b2")
    arm0, arm1, relax, mu = get("arm0"), get("arm1"), get("relax"), get("mu")
    w0, w1, w2 = [near[c] - far[c] for c in range(3)]
    s0, s1, s2 = [arm0 * near[c] + arm1 * far[c] for c in range(3, 6)]
    rate_n = n0 * w0 + n1 * w1 + n2 * w2
    rate_a = (a0 * w0 + a1 * w1) - (b0 * s0 + b1 * s1 + b2 * s2)
    rate_b = (b0 * w0 + b1 * w1 + b2 * w2) + (a0 * s0 + a1 * s1)
    trial_n = plane(impulse, 0) - relax * (rate_n + get("bias"))
    trial_a = plane(impulse, 1) - relax * rate_a
    trial_b = plane(impulse, 2) - relax * rate_b
    length = jnp.sqrt(trial_a * trial_a + trial_b * trial_b)
    inside = length <= mu * trial_n
    dead = mu * length <= -trial_n
    level = (trial_n + mu * length) / (1.0 + mu * mu)
    factor = mu * level / jnp.maximum(length, SMALLEST)
    choose = lambda kept, cone: jnp.where(inside, kept, jnp.where(dead, 0.0, cone))
    fresh = [
        choose(trial_n, level), choose(trial_a, factor * trial_a), choose(trial_b, factor * trial_b)
    ]
    for comp in range(3):
        impulse_out[comp * ROWS:(comp + 1) * ROWS, :] = fresh[comp]
    end_pulses(fresh, table, near_values, far_values)
    ghost_pulses(far_values, high_far, hot_far, up, down, left, right, left_ghost)


def shape(*dims, kind=F32):
    return jax.ShapeDtypeStruct(dims, kind)


FACES = (shape(8, FACE), shape(8, FACE))
GX_SENDS = (shape(8, MESSAGE), shape(8, MESSAGE))
VALUES = shape(8 * ROWS, 128)
PULSE = shape(8, BODY)
LEFT_OWN = pltpu.VMEM((2 * OWN_WIDE * 8, CONTACTS), BF16)
LEFT_GHOST = pltpu.VMEM((2 * GHOST_WIDE * 8, CONTACTS), BF16)


def left_list(tiles):
    return pltpu.VMEM((2 * OWN_WIDE * 8, tiles * 128), BF16)


def call(body, outs, scratch, *operands, space=pltpu.VMEM, cost=0):
    vmem = pl.BlockSpec(memory_space=pltpu.VMEM)
    return pl.pallas_call(
        body,
        out_shape=outs,
        in_specs=[pl.BlockSpec(memory_space=space)] * len(operands),
        out_specs=[vmem] * len(outs),
        scratch_shapes=scratch,
        compiler_params=pltpu.CompilerParams(vmem_limit_bytes=10 * 1024 * 1024),
    )(*operands)


def ring(value, axis, step):
    size = lax.axis_size(axis)
    return lax.ppermute(value, axis, [(i, (i + step) % size) for i in range(size)])


def along_gx(up, down):
    return ring(down, "gx", 1), ring(up, "gx", -1)


def along_gy(from_up, from_down, left, right):
    corners = from_up[:, FACE:] + from_down[:, FACE:]
    to_left = jnp.concatenate([left, corners], axis=1)
    to_right = jnp.concatenate([right, corners], axis=1)
    return ring(to_right, "gy", 1), ring(to_left, "gy", -1)


def presence():
    row_at, row_count = lax.axis_index("gx"), lax.axis_size("gx")
    col_at, col_count = lax.axis_index("gy"), lax.axis_size("gy")
    row, slot = iota((8, 128), 0), iota((8, 128), 1) // CORNER
    vertical = (row == 0) | ((row == 4) & ((slot == 0) | (slot == 2)))
    below = (row == 1) | ((row == 4) & ((slot == 1) | (slot == 3)))
    before = (row == 2) | ((row == 4) & (slot < 2))
    after = (row == 3) | ((row == 4) & (slot >= 2))
    absent = (
        (vertical & (row_at == 0)) | (below & (row_at == row_count - 1))
        | (before & (col_at == 0)) | (after & (col_at == col_count - 1))
    )
    return jnp.where(absent, 0.0, 1.0)


def shards(
    free_velocity, body_radius, face_lists, corner_lists, owner_body, other_body,
    contact_angles, contact_arms, friction, approach, start_impulse,
):
    flags = presence()
    in_rows = lambda value: value[0, 0].reshape(-1, 128)
    dma = pltpu.SemaphoreType.DMA
    (
        table, places, high_far, impulse, hot_far, near_values, far_values,
        up, down, left, right, owner, radius, faces, corners, base_rows,
    ) = call(
        prepare,
        (
            shape(len(PLANES) * ROWS, 128),
            shape(4 * ROWS, 128, kind=I32),
            shape(ROWS, 128, kind=I32),
            shape(IMPULSE_ROWS, 128),
            shape(CONTACTS, WIDE, kind=BF16),
            VALUES, VALUES,
        ) + GX_SENDS + FACES + (
            shape(ROWS, 128, kind=I32),
            shape(1, BODY),
            shape(4, FACE, kind=I32),
            shape(4, CORNER, kind=I32),
            shape(6 * OWN_TILES, 128),
        ),
        (
            pltpu.VMEM((2, CONTACTS), F32),
            pltpu.VMEM((2, CONTACTS), F32),
            pltpu.VMEM((ROWS, 128), F32),
            pltpu.VMEM((ROWS, 128), F32),
            pltpu.VMEM((ROWS, 128), I32),
            pltpu.VMEM((4 * ROWS, 128), F32),
            LEFT_GHOST,
            dma((11,)),
        ),
        contact_angles[0, 0], contact_arms[0, 0], in_rows(friction), in_rows(approach),
        in_rows(start_impulse), in_rows(owner_body), in_rows(other_body),
        body_radius[0], face_lists[0, 0], corner_lists[0, 0], in_rows(free_velocity),
        space=pltpu.HBM,
    )
    for number in range(SWEEPS + 1):
        from_up, from_down = along_gx(up, down)
        if number == 0:
            pulse, high_near, hot_near, hot_list, list_places, inverse, base = call(
                prepare_own,
                (
                    PULSE,
                    shape(ROWS, 128, kind=I32),
                    shape(CONTACTS, WIDE, kind=BF16),
                    shape(LISTED, WIDE, kind=BF16),
                    shape(16, 128, kind=I32),
                    PULSE,
                    shape(6, BODY),
                ),
                (LEFT_OWN,),
                near_values, owner, radius, faces, corners, base_rows,
            )
        else:
            (pulse,) = call(
                scatter_near, (PULSE,), (LEFT_OWN,), near_values, high_near, hot_near
            )
        from_left, from_right = along_gy(from_up, from_down, left, right)
        (own,) = call(
            scatter_far, (PULSE,), (LEFT_OWN, left_list(4)),
            flags, far_values, high_far, hot_far, pulse, list_places, hot_list, from_up, from_down,
        )
        fixed = (flags, own, inverse, base, list_places, hot_list, from_left, from_right)
        if number == SWEEPS:
            (velocity,) = call(
                settle_last, (shape(6 * OWN_TILES, 128),), (left_list(5),), *fixed
            )
            break
        velocity, up, down = call(settle, (PULSE,) + GX_SENDS, (left_list(5),), *fixed)
        from_up, from_down = along_gx(up, down)
        near, left, right = call(
            gather_near, (shape(6 * ROWS, 128),) + FACES, (), velocity, places, list_places
        )
        from_left, from_right = along_gy(from_up, from_down, left, right)
        (far,) = call(
            gather_far, (shape(6 * ROWS, 128),), (), flags, velocity, places, from_up, from_down
        )
        impulse, near_values, far_values, up, down, left, right = call(
            sweep, (shape(IMPULSE_ROWS, 128), VALUES, VALUES) + GX_SENDS + FACES, (LEFT_GHOST,),
            flags, near, far, table, places, high_far, hot_far, impulse, from_left, from_right,
        )
    return velocity.reshape(1, 1, 6, BODY), impulse.reshape(1, 1, 3, CONTACTS)

def solution(mesh):
    in_specs = (
        P("gx", "gy", None, None),
        P("gx", "gy", None),
        P("gx", "gy", None, None),
        P("gx", "gy", None, None),
        P("gx", "gy", None),
        P("gx", "gy", None),
        P("gx", "gy", None, None),
        P("gx", "gy", None, None),
        P("gx", "gy", None),
        P("gx", "gy", None),
        P("gx", "gy", None, None),
    )
    out_specs = (P("gx", "gy", None, None), P("gx", "gy", None, None))
    return jax.shard_map(shards, mesh=mesh, in_specs=in_specs, out_specs=out_specs, check_vma=False)
```

time: 149 us -> 129 us (0.87)
  starting transfers between devices: 58.9 us -> 30.5 us
  waiting for transfers between devices: 46.7 us -> 62.8 us
  local copies, waits for them, and re-layouts: 11.7 us -> 8.04 us
  Pallas kernels: 29.6 us -> 26.4 us
    ppermute x36, starting transfers between devices: 58.9 us -> 30.5 us  [ring(): lax.ppermute(value, axis, [(i, (i + step) % size) for i in range(size)])]
    ppermute x36, waiting for transfers between devices: 46.7 us -> 62.8 us  [ring(): lax.ppermute(value, axis, [(i, (i + step) % size) for i in range(size)])]
    unnamed x27 -> x22, local copies, waits for them, and re-layouts: 11.7 us -> 8.04 us
    pallas_call x19 -> x28, Pallas kernels: 29.6 us -> 26.4 us  [call(): pl.pallas_call(body, out_shape=outs, in_specs=[pl.BlockSpec(memory_space=...]
  transfers between devices with their start and end apart: 36 -> 36, of which waited for: 28 -> 23; matrix products, arithmetic and copies ran while one was open for 1% -> 0% of each run, Pallas kernels for 0% -> 14%
where the time goes in v2:
time: 129 us
  waiting for transfers between devices  62.8 us (49%)
  starting transfers between devices  30.5 us (24%)
  Pallas kernels  26.4 us (20%)
  local copies, waits for them, and re-layouts  8.04 us (6%)
    ppermute x36, waiting for transfers between devices, ring(): lax.ppermute(value, axis, [(i, (i + step) % size) for i in range(size)])  62.8 us
    ppermute x36, starting transfers between devices, ring(): lax.ppermute(value, axis, [(i, (i + step) % size) for i in range(size)])  30.5 us
    pallas_call x28, Pallas kernels, call(): pl.pallas_call(body, out_shape=outs, in_specs=[pl.BlockSpec(memory_space=...  26.4 us
    unnamed x22, local copies, waits for them, and re-layouts  8.04 us
  transfers between devices with their start and end apart: 36, of which 23 were waited for; matrix products, arithmetic and copies ran while one was open for 0% of the time, Pallas kernels for 14%

profile of v2, /device:TPU:25, one launch (start us, length us, event | category | flops | bytes accessed | tf_op | source)
XLA Modules:
  0.0 128.8 jit_solution(12566507648317229716)
XLA Ops:
  8.7 2.0 %shard_map.122 = (f32[416,128]{1,0:T(8,128)S(1)}, s32[128,128]{1,0:T(8,128)S(1)}, s32[32,128]{1,0:T(8,128)S(1)}, f32[96,128]{1,0:T(8,128)S(1)}, bf16[4096,256]{1...) custom-call(f32[2,4096]{1,0:T(2,128)S(1)} %bitcast.15, ...), custom_call_target="tpu_custom_call" | custom-call | tf_op jit(solution)/shard_map/pallas_call | solution.py:430
  10.7 2.2 %collective-permute-start = (f32[8,384]{1,0:T(8,128)S(1)}, f32[8,384]{1,0:T(8,128)S(1)}, u32[]{:S(2)}, u32[]{:S(2)}) collective-permute-start(f32[8,384]{1,0:T(8,128)S(1)} %get-tuple-element.89), channel_id=1, source_target_pairs={{0,32},{32,64},{64,96},{96,128},{128,160},{160,192},{192,224},{224... | collective-permute-start | bytes 36872 | tf_op jit(solution)/shard_map/ppermute | solution.py:442
  13.8 3.5 %collective-permute-done.1.from_down = f32[8,384]{1,0:T(8,128)S(1)} collective-permute-done((f32[8,384]{1,0:T(8,128)S(1)}, f32[8,384]{1,0:T(8,128)S(1)}, u32[]{:S(2)}, u32[]{:S(2)}) %collective-permute-start.1) | collective-permute-done | bytes 12320 | tf_op jit(solution)/shard_map/ppermute | solution.py:442
  17.3 6.0 %collective-permute-start.3 = (f32[8,384]{1,0:T(8,128)S(1)}, f32[8,384]{1,0:T(8,128)S(1)}, u32[]{:S(2)}, u32[]{:S(2)}) collective-permute-start(f32[8,384]{1,0:T(8,128)S(1)} %get-tuple-element.172), channel_id=1, source_target_pairs={{0,31},{1,0},{2,1},{3,2},{4,3},{5,4},{6,5},{7,6},{8,7},{9,8},{10,9... | collective-permute-start | bytes 36872 | tf_op jit(solution)/shard_map/ppermute | solution.py:442
  23.4 1.4 %shard_map.123 = (f32[8,2048]{1,0:T(8,128)S(1)}, s32[32,128]{1,0:T(8,128)S(1)}, bf16[4096,256]{1,0:T(8,128)(2,1)S(1)}, bf16[1152,256]{1,0:T(8,128)(2,1)S(1)}, s3...) custom-call(f32[256,128]{1,0:T(8,128)S(1)} %get-tuple-element.80.near_values, ...), custom_call_target="tpu_custom_call" | custom-call | tf_op jit(solution)/shard_map/pallas_call | solution.py:430
  25.6 3.7 %collective-permute-done.2.from_left = f32[8,384]{1,0:T(8,128)S(1)} collective-permute-done((f32[8,384]{1,0:T(8,128)S(1)}, f32[8,384]{1,0:T(8,128)S(1)}, u32[]{:S(2)}, u32[]{:S(2)}) %collective-permute-start.2) | collective-permute-done | bytes 12320 | tf_op jit(solution)/shard_map/ppermute | solution.py:442
  29.7 1.4 %collective-permute-start.4 = (f32[8,384]{1,0:T(8,128)S(1)}, f32[8,384]{1,0:T(8,128)S(1)}, u32[]{:S(2)}, u32[]{:S(2)}) collective-permute-start(f32[8,384]{1,0:T(8,128)S(1)} %get-tuple-element.98), channel_id=1, source_target_pairs={{0,32},{32,64},{64,96},{96,128},{128,160},{160,192},{192,224},{224... | collective-permute-start | bytes 36872 | tf_op jit(solution)/shard_map/ppermute | solution.py:442
  31.2 1.2 shard_map.126
  32.4 3.1 %collective-permute-done.5.from_down = f32[8,384]{1,0:T(8,128)S(1)} collective-permute-done((f32[8,384]{1,0:T(8,128)S(1)}, f32[8,384]{1,0:T(8,128)S(1)}, u32[]{:S(2)}, u32[]{:S(2)}) %collective-permute-start.5) | collective-permute-done | bytes 12320 | tf_op jit(solution)/shard_map/ppermute | solution.py:442
  35.8 1.1 collective-permute-start.6
  37.0 1.4 %shard_map.127.far_ref = f32[192,128]{1,0:T(8,128)S(1)} custom-call(f32[8,128]{1,0:T(8,128)S(1)} %fusion.7.flags, f32[8,2048]{1,0:T(8,128)S(1)} %get-tuple-element.95.velocity, s32[128,128]{1,0:T(8,128)S(1)} %get-tuple-element.96.places, f32[8,384]{1,0:T(8,128)S(1)} %collective-permute-done.4.from_up, f32[8,384]{1,0:T(8,128)S(1)} %collective-permute-done.5.from_down), custom_call_target="tpu_custom_call" | custom-call | tf_op jit(solution)/shard_map/pallas_call | solution.py:430
  38.4 3.3 %collective-permute-done.6.from_left = f32[8,384]{1,0:T(8,128)S(1)} collective-permute-done((f32[8,384]{1,0:T(8,128)S(1)}, f32[8,384]{1,0:T(8,128)S(1)}, u32[]{:S(2)}, u32[]{:S(2)}) %collective-permute-start.6) | collective-permute-done | bytes 12320 | tf_op jit(solution)/shard_map/ppermute | solution.py:442
  42.4 1.5 %collective-permute-start.8 = (f32[8,384]{1,0:T(8,128)S(1)}, f32[8,384]{1,0:T(8,128)S(1)}, u32[]{:S(2)}, u32[]{:S(2)}) collective-permute-start(f32[8,384]{1,0:T(8,128)S(1)} %get-tuple-element.108), channel_id=1, source_target_pairs={{0,32},{32,64},{64,96},{96,128},{128,160},{160,192},{192,224},{224... | collective-permute-start | bytes 36872 | tf_op jit(solution)/shard_map/ppermute | solution.py:442
  44.8 3.5 %collective-permute-done.9.from_down = f32[8,384]{1,0:T(8,128)S(1)} collective-permute-done((f32[8,384]{1,0:T(8,128)S(1)}, f32[8,384]{1,0:T(8,128)S(1)}, u32[]{:S(2)}, u32[]{:S(2)}) %collective-permute-start.9) | collective-permute-done | bytes 12320 | tf_op jit(solution)/shard_map/ppermute | solution.py:442
  48.3 1.5 %collective-permute-start.10 = (f32[8,384]{1,0:T(8,128)S(1)}, f32[8,384]{1,0:T(8,128)S(1)}, u32[]{:S(2)}, u32[]{:S(2)}) collective-permute-start(f32[8,384]{1,0:T(8,128)S(1)} %get-tuple-element.169), channel_id=1, source_target_pairs={{0,1},{1,2},{2,3},{3,4},{4,5},{5,6},{6,7},{7,8},{8,9},{9,10},{10,1... | collective-permute-start | bytes 36872 | tf_op jit(solution)/shard_map/ppermute | solution.py:442
  51.2 3.2 %collective-permute-done.10.from_left = f32[8,384]{1,0:T(8,128)S(1)} collective-permute-done((f32[8,384]{1,0:T(8,128)S(1)}, f32[8,384]{1,0:T(8,128)S(1)}, u32[]{:S(2)}, u32[]{:S(2)}) %collective-permute-start.10) | collective-permute-done | bytes 12320 | tf_op jit(solution)/shard_map/ppermute | solution.py:442
  54.9 1.3 collective-permute-start.12
  56.1 1.2 shard_map.132
  57.4 3.1 %collective-permute-done.13.from_down = f32[8,384]{1,0:T(8,128)S(1)} collective-permute-done((f32[8,384]{1,0:T(8,128)S(1)}, f32[8,384]{1,0:T(8,128)S(1)}, u32[]{:S(2)}, u32[]{:S(2)}) %collective-permute-start.13) | collective-permute-done | bytes 12320 | tf_op jit(solution)/shard_map/ppermute | solution.py:442
  60.5 1.5 %collective-permute-start.14 = (f32[8,384]{1,0:T(8,128)S(1)}, f32[8,384]{1,0:T(8,128)S(1)}, u32[]{:S(2)}, u32[]{:S(2)}) collective-permute-start(f32[8,384]{1,0:T(8,128)S(1)} %get-tuple-element.167), channel_id=1, source_target_pairs={{0,1},{1,2},{2,3},{3,4},{4,5},{5,6},{6,7},{7,8},{8,9},{9,10},{10,1... | collective-permute-start | bytes 36872 | tf_op jit(solution)/shard_map/ppermute | solution.py:442
  61.9 1.4 %shard_map.133.far_ref = f32[192,128]{1,0:T(8,128)S(1)} custom-call(f32[8,128]{1,0:T(8,128)S(1)} %fusion.7.flags, f32[8,2048]{1,0:T(8,128)S(1)} %get-tuple-element.112.velocity, s32[128,128]{1,0:T(8,128)S(1)} %get-tuple-element.96.places, f32[8,384]{1,0:T(8,128)S(1)} %collective-permute-done.12.from_up, f32[8,384]{1,0:T(8,128)S(1)} %collective-permute-done.13.from_down), custom_call_target="tpu_custom_call" | custom-call | tf_op jit(solution)/shard_map/pallas_call | solution.py:430
  63.3 3.1 %collective-permute-done.14.from_left = f32[8,384]{1,0:T(8,128)S(1)} collective-permute-done((f32[8,384]{1,0:T(8,128)S(1)}, f32[8,384]{1,0:T(8,128)S(1)}, u32[]{:S(2)}, u32[]{:S(2)}) %collective-permute-start.14) | collective-permute-done | bytes 12320 | tf_op jit(solution)/shard_map/ppermute | solution.py:442
  67.2 1.3 collective-permute-start.16
  69.3 3.5 %collective-permute-done.17.from_down = f32[8,384]{1,0:T(8,128)S(1)} collective-permute-done((f32[8,384]{1,0:T(8,128)S(1)}, f32[8,384]{1,0:T(8,128)S(1)}, u32[]{:S(2)}, u32[]{:S(2)}) %collective-permute-start.17) | collective-permute-done | bytes 12320 | tf_op jit(solution)/shard_map/ppermute | solution.py:442
  72.8 1.5 %collective-permute-start.18 = (f32[8,384]{1,0:T(8,128)S(1)}, f32[8,384]{1,0:T(8,128)S(1)}, u32[]{:S(2)}, u32[]{:S(2)}) collective-permute-start(f32[8,384]{1,0:T(8,128)S(1)} %get-tuple-element.165), channel_id=1, source_target_pairs={{0,1},{1,2},{2,3},{3,4},{4,5},{5,6},{6,7},{7,8},{8,9},{9,10},{10,1... | collective-permute-start | bytes 36872 | tf_op jit(solution)/shard_map/ppermute | solution.py:442
  75.7 3.0 %collective-permute-done.18.from_left = f32[8,384]{1,0:T(8,128)S(1)} collective-permute-done((f32[8,384]{1,0:T(8,128)S(1)}, f32[8,384]{1,0:T(8,128)S(1)}, u32[]{:S(2)}, u32[]{:S(2)}) %collective-permute-start.18) | collective-permute-done | bytes 12320 | tf_op jit(solution)/shard_map/ppermute | solution.py:442
  79.2 1.3 collective-permute-start.20
  80.4 1.2 shard_map.138
  81.6 3.1 %collective-permute-done.21.from_down = f32[8,384]{1,0:T(8,128)S(1)} collective-permute-done((f32[8,384]{1,0:T(8,128)S(1)}, f32[8,384]{1,0:T(8,128)S(1)}, u32[]{:S(2)}, u32[]{:S(2)}) %collective-permute-start.21) | collective-permute-done | bytes 12320 | tf_op jit(solution)/shard_map/ppermute | solution.py:442
  84.8 1.5 %collective-permute-start.22 = (f32[8,384]{1,0:T(8,128)S(1)}, f32[8,384]{1,0:T(8,128)S(1)}, u32[]{:S(2)}, u32[]{:S(2)}) collective-permute-start(f32[8,384]{1,0:T(8,128)S(1)} %get-tuple-element.163), channel_id=1, source_target_pairs={{0,1},{1,2},{2,3},{3,4},{4,5},{5,6},{6,7},{7,8},{8,9},{9,10},{10,1... | collective-permute-start | bytes 36872 | tf_op jit(solution)/shard_map/ppermute | solution.py:442
  86.2 1.4 %shard_map.139.far_ref = f32[192,128]{1,0:T(8,128)S(1)} custom-call(f32[8,128]{1,0:T(8,128)S(1)} %fusion.7.flags, f32[8,2048]{1,0:T(8,128)S(1)} %get-tuple-element.125.velocity, s32[128,128]{1,0:T(8,128)S(1)} %get-tuple-element.96.places, f32[8,384]{1,0:T(8,128)S(1)} %collective-permute-done.20.from_up, f32[8,384]{1,0:T(8,128)S(1)} %collective-permute-done.21.from_down), custom_call_target="tpu_custom_call" | custom-call | tf_op jit(solution)/shard_map/pallas_call | solution.py:430
  87.6 3.1 %collective-permute-done.22.from_left = f32[8,384]{1,0:T(8,128)S(1)} collective-permute-done((f32[8,384]{1,0:T(8,128)S(1)}, f32[8,384]{1,0:T(8,128)S(1)}, u32[]{:S(2)}, u32[]{:S(2)}) %collective-permute-start.22) | collective-permute-done | bytes 12320 | tf_op jit(solution)/shard_map/ppermute | solution.py:442
  91.5 1.3 collective-permute-start.24
  93.5 3.5 %collective-permute-done.25.from_down = f32[8,384]{1,0:T(8,128)S(1)} collective-permute-done((f32[8,384]{1,0:T(8,128)S(1)}, f32[8,384]{1,0:T(8,128)S(1)}, u32[]{:S(2)}, u32[]{:S(2)}) %collective-permute-start.25) | collective-permute-done | bytes 12320 | tf_op jit(solution)/shard_map/ppermute | solution.py:442
  97.1 1.5 %collective-permute-start.26 = (f32[8,384]{1,0:T(8,128)S(1)}, f32[8,384]{1,0:T(8,128)S(1)}, u32[]{:S(2)}, u32[]{:S(2)}) collective-permute-start(f32[8,384]{1,0:T(8,128)S(1)} %get-tuple-element.161), channel_id=1, source_target_pairs={{0,1},{1,2},{2,3},{3,4},{4,5},{5,6},{6,7},{7,8},{8,9},{9,10},{10,1... | collective-permute-start | bytes 36872 | tf_op jit(solution)/shard_map/ppermute | solution.py:442
  99.9 3.3 %collective-permute-done.26.from_left = f32[8,384]{1,0:T(8,128)S(1)} collective-permute-done((f32[8,384]{1,0:T(8,128)S(1)}, f32[8,384]{1,0:T(8,128)S(1)}, u32[]{:S(2)}, u32[]{:S(2)}) %collective-permute-start.26) | collective-permute-done | bytes 12320 | tf_op jit(solution)/shard_map/ppermute | solution.py:442
  103.7 1.3 collective-permute-start.28
  104.9 1.2 shard_map.144
  106.1 3.1 %collective-permute-done.29.from_down = f32[8,384]{1,0:T(8,128)S(1)} collective-permute-done((f32[8,384]{1,0:T(8,128)S(1)}, f32[8,384]{1,0:T(8,128)S(1)}, u32[]{:S(2)}, u32[]{:S(2)}) %collective-permute-start.29) | collective-permute-done | bytes 12320 | tf_op jit(solution)/shard_map/ppermute | solution.py:442
  109.3 1.5 %collective-permute-start.30 = (f32[8,384]{1,0:T(8,128)S(1)}, f32[8,384]{1,0:T(8,128)S(1)}, u32[]{:S(2)}, u32[]{:S(2)}) collective-permute-start(f32[8,384]{1,0:T(8,128)S(1)} %get-tuple-element.159), channel_id=1, source_target_pairs={{0,1},{1,2},{2,3},{3,4},{4,5},{5,6},{6,7},{7,8},{8,9},{9,10},{10,1... | collective-permute-start | bytes 36872 | tf_op jit(solution)/shard_map/ppermute | solution.py:442
  110.7 1.4 %shard_map.145.far_ref = f32[192,128]{1,0:T(8,128)S(1)} custom-call(f32[8,128]{1,0:T(8,128)S(1)} %fusion.7.flags, f32[8,2048]{1,0:T(8,128)S(1)} %get-tuple-element.138.velocity, s32[128,128]{1,0:T(8,128)S(1)} %get-tuple-element.96.places, f32[8,384]{1,0:T(8,128)S(1)} %collective-permute-done.28.from_up, f32[8,384]{1,0:T(8,128)S(1)} %collective-permute-done.29.from_down), custom_call_target="tpu_custom_call" | custom-call | tf_op jit(solution)/shard_map/pallas_call | solution.py:430
  112.1 3.1 %collective-permute-done.30.from_left = f32[8,384]{1,0:T(8,128)S(1)} collective-permute-done((f32[8,384]{1,0:T(8,128)S(1)}, f32[8,384]{1,0:T(8,128)S(1)}, u32[]{:S(2)}, u32[]{:S(2)}) %collective-permute-start.30) | collective-permute-done | bytes 12320 | tf_op jit(solution)/shard_map/ppermute | solution.py:442
  115.2 1.2 shard_map.146
  116.4 1.2 collective-permute-start.32
  118.5 3.5 %collective-permute-done.33.from_down = f32[8,384]{1,0:T(8,128)S(1)} collective-permute-done((f32[8,384]{1,0:T(8,128)S(1)}, f32[8,384]{1,0:T(8,128)S(1)}, u32[]{:S(2)}, u32[]{:S(2)}) %collective-permute-start.33) | collective-permute-done | bytes 12320 | tf_op jit(solution)/shard_map/ppermute | solution.py:442
  122.0 1.5 %collective-permute-start.34 = (f32[8,384]{1,0:T(8,128)S(1)}, f32[8,384]{1,0:T(8,128)S(1)}, u32[]{:S(2)}, u32[]{:S(2)}) collective-permute-start(f32[8,384]{1,0:T(8,128)S(1)} %get-tuple-element.157), channel_id=1, source_target_pairs={{0,1},{1,2},{2,3},{3,4},{4,5},{5,6},{6,7},{7,8},{8,9},{9,10},{10,1... | collective-permute-start | bytes 36872 | tf_op jit(solution)/shard_map/ppermute | solution.py:442
  124.9 3.1 %collective-permute-done.34.from_left = f32[8,384]{1,0:T(8,128)S(1)} collective-permute-done((f32[8,384]{1,0:T(8,128)S(1)}, f32[8,384]{1,0:T(8,128)S(1)}, u32[]{:S(2)}, u32[]{:S(2)}) %collective-permute-start.34) | collective-permute-done | bytes 12320 | tf_op jit(solution)/shard_map/ppermute | solution.py:442
  128.0 0.9 shard_map.149
  (98 shorter events, 23.1 us)
Async XLA Ops:
  0.6 0.8 copy-start
  1.4 0.8 copy-start.1
  2.2 0.8 copy-start.2
  3.0 0.8 copy-start.3
  3.7 0.7 copy-start.4
  4.5 0.7 copy-start.5
  5.2 0.7 copy-start.6
  5.9 0.7 copy-start.7
  6.6 0.7 copy-start.8
  7.3 0.7 copy-start.9
  8.0 0.7 copy-start.10
  10.7 3.1 %collective-permute-start = (f32[8,384]{1,0:T(8,128)S(1)}, f32[8,384]{1,0:T(8,128)S(1)}, u32[]{:S(2)}, u32[]{:S(2)}) collective-permute-start(f32[8,384]{1,0:T(8,128)S(1)} %get-tuple-element.89), channel_id=1, source_target_pairs={{0,32},{32,64},{64,96},{96,128},{128,160},{160,192},{192,224},{224... | collective-permute-start | bytes 36872 | tf_op jit(solution)/shard_map/ppermute | solution.py:442
  12.9 4.3 %collective-permute-start.1 = (f32[8,384]{1,0:T(8,128)S(1)}, f32[8,384]{1,0:T(8,128)S(1)}, u32[]{:S(2)}, u32[]{:S(2)}) collective-permute-start(f32[8,384]{1,0:T(8,128)S(1)} %get-tuple-element.90), channel_id=1, source_target_pairs={{0,224},{32,0},{64,32},{96,64},{128,96},{160,128},{192,160},{224,1... | collective-permute-start | bytes 36872 | tf_op jit(solution)/shard_map/ppermute | solution.py:442
  17.3 8.3 %collective-permute-start.3 = (f32[8,384]{1,0:T(8,128)S(1)}, f32[8,384]{1,0:T(8,128)S(1)}, u32[]{:S(2)}, u32[]{:S(2)}) collective-permute-start(f32[8,384]{1,0:T(8,128)S(1)} %get-tuple-element.172), channel_id=1, source_target_pairs={{0,31},{1,0},{2,1},{3,2},{4,3},{5,4},{6,5},{7,6},{8,7},{9,8},{10,9... | collective-permute-start | bytes 36872 | tf_op jit(solution)/shard_map/ppermute | solution.py:442
  23.3 5.9 %collective-permute-start.2 = (f32[8,384]{1,0:T(8,128)S(1)}, f32[8,384]{1,0:T(8,128)S(1)}, u32[]{:S(2)}, u32[]{:S(2)}) collective-permute-start(f32[8,384]{1,0:T(8,128)S(1)} %get-tuple-element.173), channel_id=1, source_target_pairs={{0,1},{1,2},{2,3},{3,4},{4,5},{5,6},{6,7},{7,8},{8,9},{9,10},{10,1... | collective-permute-start | bytes 36872 | tf_op jit(solution)/shard_map/ppermute | solution.py:442
  29.7 2.7 %collective-permute-start.4 = (f32[8,384]{1,0:T(8,128)S(1)}, f32[8,384]{1,0:T(8,128)S(1)}, u32[]{:S(2)}, u32[]{:S(2)}) collective-permute-start(f32[8,384]{1,0:T(8,128)S(1)} %get-tuple-element.98), channel_id=1, source_target_pairs={{0,32},{32,64},{64,96},{96,128},{128,160},{160,192},{192,224},{224... | collective-permute-start | bytes 36872 | tf_op jit(solution)/shard_map/ppermute | solution.py:442
  31.2 4.3 %collective-permute-start.5 = (f32[8,384]{1,0:T(8,128)S(1)}, f32[8,384]{1,0:T(8,128)S(1)}, u32[]{:S(2)}, u32[]{:S(2)}) collective-permute-start(f32[8,384]{1,0:T(8,128)S(1)} %get-tuple-element.99), channel_id=1, source_target_pairs={{0,224},{32,0},{64,32},{96,64},{128,96},{160,128},{192,160},{224,1... | collective-permute-start | bytes 36872 | tf_op jit(solution)/shard_map/ppermute | solution.py:442
  35.5 2.9 %collective-permute-start.7 = (f32[8,384]{1,0:T(8,128)S(1)}, f32[8,384]{1,0:T(8,128)S(1)}, u32[]{:S(2)}, u32[]{:S(2)}) collective-permute-start(f32[8,384]{1,0:T(8,128)S(1)} %get-tuple-element.170), channel_id=1, source_target_pairs={{0,31},{1,0},{2,1},{3,2},{4,3},{5,4},{6,5},{7,6},{8,7},{9,8},{10,9... | collective-permute-start | bytes 36872 | tf_op jit(solution)/shard_map/ppermute | solution.py:442
  35.8 5.9 %collective-permute-start.6 = (f32[8,384]{1,0:T(8,128)S(1)}, f32[8,384]{1,0:T(8,128)S(1)}, u32[]{:S(2)}, u32[]{:S(2)}) collective-permute-start(f32[8,384]{1,0:T(8,128)S(1)} %get-tuple-element.171), channel_id=1, source_target_pairs={{0,1},{1,2},{2,3},{3,4},{4,5},{5,6},{6,7},{7,8},{8,9},{9,10},{10,1... | collective-permute-start | bytes 36872 | tf_op jit(solution)/shard_map/ppermute | solution.py:442
  42.4 2.4 %collective-permute-start.8 = (f32[8,384]{1,0:T(8,128)S(1)}, f32[8,384]{1,0:T(8,128)S(1)}, u32[]{:S(2)}, u32[]{:S(2)}) collective-permute-start(f32[8,384]{1,0:T(8,128)S(1)} %get-tuple-element.108), channel_id=1, source_target_pairs={{0,32},{32,64},{64,96},{96,128},{128,160},{160,192},{192,224},{224... | collective-permute-start | bytes 36872 | tf_op jit(solution)/shard_map/ppermute | solution.py:442
  44.0 4.3 %collective-permute-start.9 = (f32[8,384]{1,0:T(8,128)S(1)}, f32[8,384]{1,0:T(8,128)S(1)}, u32[]{:S(2)}, u32[]{:S(2)}) collective-permute-start(f32[8,384]{1,0:T(8,128)S(1)} %get-tuple-element.109), channel_id=1, source_target_pairs={{0,224},{32,0},{64,32},{96,64},{128,96},{160,128},{192,160},{224,1... | collective-permute-start | bytes 36872 | tf_op jit(solution)/shard_map/ppermute | solution.py:442
  48.3 2.9 %collective-permute-start.11 = (f32[8,384]{1,0:T(8,128)S(1)}, f32[8,384]{1,0:T(8,128)S(1)}, u32[]{:S(2)}, u32[]{:S(2)}) collective-permute-start(f32[8,384]{1,0:T(8,128)S(1)} %get-tuple-element.168), channel_id=1, source_target_pairs={{0,31},{1,0},{2,1},{3,2},{4,3},{5,4},{6,5},{7,6},{8,7},{9,8},{10,9... | collective-permute-start | bytes 36872 | tf_op jit(solution)/shard_map/ppermute | solution.py:442
  48.3 6.1 %collective-permute-start.10 = (f32[8,384]{1,0:T(8,128)S(1)}, f32[8,384]{1,0:T(8,128)S(1)}, u32[]{:S(2)}, u32[]{:S(2)}) collective-permute-start(f32[8,384]{1,0:T(8,128)S(1)} %get-tuple-element.169), channel_id=1, source_target_pairs={{0,1},{1,2},{2,3},{3,4},{4,5},{5,6},{6,7},{7,8},{8,9},{9,10},{10,1... | collective-permute-start | bytes 36872 | tf_op jit(solution)/shard_map/ppermute | solution.py:442
  54.9 2.5 %collective-permute-start.12 = (f32[8,384]{1,0:T(8,128)S(1)}, f32[8,384]{1,0:T(8,128)S(1)}, u32[]{:S(2)}, u32[]{:S(2)}) collective-permute-start(f32[8,384]{1,0:T(8,128)S(1)} %get-tuple-element.114), channel_id=1, source_target_pairs={{0,32},{32,64},{64,96},{96,128},{128,160},{160,192},{192,224},{224... | collective-permute-start | bytes 36872 | tf_op jit(solution)/shard_map/ppermute | solution.py:442
  56.1 4.3 %collective-permute-start.13 = (f32[8,384]{1,0:T(8,128)S(1)}, f32[8,384]{1,0:T(8,128)S(1)}, u32[]{:S(2)}, u32[]{:S(2)}) collective-permute-start(f32[8,384]{1,0:T(8,128)S(1)} %get-tuple-element.115), channel_id=1, source_target_pairs={{0,224},{32,0},{64,32},{96,64},{128,96},{160,128},{192,160},{224,1... | collective-permute-start | bytes 36872 | tf_op jit(solution)/shard_map/ppermute | solution.py:442
  60.5 2.9 %collective-permute-start.15 = (f32[8,384]{1,0:T(8,128)S(1)}, f32[8,384]{1,0:T(8,128)S(1)}, u32[]{:S(2)}, u32[]{:S(2)}) collective-permute-start(f32[8,384]{1,0:T(8,128)S(1)} %get-tuple-element.166), channel_id=1, source_target_pairs={{0,31},{1,0},{2,1},{3,2},{4,3},{5,4},{6,5},{7,6},{8,7},{9,8},{10,9... | collective-permute-start | bytes 36872 | tf_op jit(solution)/shard_map/ppermute | solution.py:442
  60.5 5.9 %collective-permute-start.14 = (f32[8,384]{1,0:T(8,128)S(1)}, f32[8,384]{1,0:T(8,128)S(1)}, u32[]{:S(2)}, u32[]{:S(2)}) collective-permute-start(f32[8,384]{1,0:T(8,128)S(1)} %get-tuple-element.167), channel_id=1, source_target_pairs={{0,1},{1,2},{2,3},{3,4},{4,5},{5,6},{6,7},{7,8},{8,9},{9,10},{10,1... | collective-permute-start | bytes 36872 | tf_op jit(solution)/shard_map/ppermute | solution.py:442
  67.2 2.1 %collective-permute-start.16 = (f32[8,384]{1,0:T(8,128)S(1)}, f32[8,384]{1,0:T(8,128)S(1)}, u32[]{:S(2)}, u32[]{:S(2)}) collective-permute-start(f32[8,384]{1,0:T(8,128)S(1)} %get-tuple-element.121), channel_id=1, source_target_pairs={{0,32},{32,64},{64,96},{96,128},{128,160},{160,192},{192,224},{224... | collective-permute-start | bytes 36872 | tf_op jit(solution)/shard_map/ppermute | solution.py:442
  68.4 4.3 %collective-permute-start.17 = (f32[8,384]{1,0:T(8,128)S(1)}, f32[8,384]{1,0:T(8,128)S(1)}, u32[]{:S(2)}, u32[]{:S(2)}) collective-permute-start(f32[8,384]{1,0:T(8,128)S(1)} %get-tuple-element.122), channel_id=1, source_target_pairs={{0,224},{32,0},{64,32},{96,64},{128,96},{160,128},{192,160},{224,1... | collective-permute-start | bytes 36872 | tf_op jit(solution)/shard_map/ppermute | solution.py:442
  72.8 2.9 %collective-permute-start.19 = (f32[8,384]{1,0:T(8,128)S(1)}, f32[8,384]{1,0:T(8,128)S(1)}, u32[]{:S(2)}, u32[]{:S(2)}) collective-permute-start(f32[8,384]{1,0:T(8,128)S(1)} %get-tuple-element.164), channel_id=1, source_target_pairs={{0,31},{1,0},{2,1},{3,2},{4,3},{5,4},{6,5},{7,6},{8,7},{9,8},{10,9... | collective-permute-start | bytes 36872 | tf_op jit(solution)/shard_map/ppermute | solution.py:442
  72.8 5.9 %collective-permute-start.18 = (f32[8,384]{1,0:T(8,128)S(1)}, f32[8,384]{1,0:T(8,128)S(1)}, u32[]{:S(2)}, u32[]{:S(2)}) collective-permute-start(f32[8,384]{1,0:T(8,128)S(1)} %get-tuple-element.165), channel_id=1, source_target_pairs={{0,1},{1,2},{2,3},{3,4},{4,5},{5,6},{6,7},{7,8},{8,9},{9,10},{10,1... | collective-permute-start | bytes 36872 | tf_op jit(solution)/shard_map/ppermute | solution.py:442
  79.2 2.5 %collective-permute-start.20 = (f32[8,384]{1,0:T(8,128)S(1)}, f32[8,384]{1,0:T(8,128)S(1)}, u32[]{:S(2)}, u32[]{:S(2)}) collective-permute-start(f32[8,384]{1,0:T(8,128)S(1)} %get-tuple-element.127), channel_id=1, source_target_pairs={{0,32},{32,64},{64,96},{96,128},{128,160},{160,192},{192,224},{224... | collective-permute-start | bytes 36872 | tf_op jit(solution)/shard_map/ppermute | solution.py:442
  80.4 4.3 %collective-permute-start.21 = (f32[8,384]{1,0:T(8,128)S(1)}, f32[8,384]{1,0:T(8,128)S(1)}, u32[]{:S(2)}, u32[]{:S(2)}) collective-permute-start(f32[8,384]{1,0:T(8,128)S(1)} %get-tuple-element.128), channel_id=1, source_target_pairs={{0,224},{32,0},{64,32},{96,64},{128,96},{160,128},{192,160},{224,1... | collective-permute-start | bytes 36872 | tf_op jit(solution)/shard_map/ppermute | solution.py:442
  84.8 2.9 %collective-permute-start.23 = (f32[8,384]{1,0:T(8,128)S(1)}, f32[8,384]{1,0:T(8,128)S(1)}, u32[]{:S(2)}, u32[]{:S(2)}) collective-permute-start(f32[8,384]{1,0:T(8,128)S(1)} %get-tuple-element.162), channel_id=1, source_target_pairs={{0,31},{1,0},{2,1},{3,2},{4,3},{5,4},{6,5},{7,6},{8,7},{9,8},{10,9... | collective-permute-start | bytes 36872 | tf_op jit(solution)/shard_map/ppermute | solution.py:442
  84.8 5.9 %collective-permute-start.22 = (f32[8,384]{1,0:T(8,128)S(1)}, f32[8,384]{1,0:T(8,128)S(1)}, u32[]{:S(2)}, u32[]{:S(2)}) collective-permute-start(f32[8,384]{1,0:T(8,128)S(1)} %get-tuple-element.163), channel_id=1, source_target_pairs={{0,1},{1,2},{2,3},{3,4},{4,5},{5,6},{6,7},{7,8},{8,9},{9,10},{10,1... | collective-permute-start | bytes 36872 | tf_op jit(solution)/shard_map/ppermute | solution.py:442
  91.5 2.1 %collective-permute-start.24 = (f32[8,384]{1,0:T(8,128)S(1)}, f32[8,384]{1,0:T(8,128)S(1)}, u32[]{:S(2)}, u32[]{:S(2)}) collective-permute-start(f32[8,384]{1,0:T(8,128)S(1)} %get-tuple-element.134), channel_id=1, source_target_pairs={{0,32},{32,64},{64,96},{96,128},{128,160},{160,192},{192,224},{224... | collective-permute-start | bytes 36872 | tf_op jit(solution)/shard_map/ppermute | solution.py:442
  92.7 4.3 %collective-permute-start.25 = (f32[8,384]{1,0:T(8,128)S(1)}, f32[8,384]{1,0:T(8,128)S(1)}, u32[]{:S(2)}, u32[]{:S(2)}) collective-permute-start(f32[8,384]{1,0:T(8,128)S(1)} %get-tuple-element.135), channel_id=1, source_target_pairs={{0,224},{32,0},{64,32},{96,64},{128,96},{160,128},{192,160},{224,1... | collective-permute-start | bytes 36872 | tf_op jit(solution)/shard_map/ppermute | solution.py:442
  97.0 2.9 %collective-permute-start.27 = (f32[8,384]{1,0:T(8,128)S(1)}, f32[8,384]{1,0:T(8,128)S(1)}, u32[]{:S(2)}, u32[]{:S(2)}) collective-permute-start(f32[8,384]{1,0:T(8,128)S(1)} %get-tuple-element.160), channel_id=1, source_target_pairs={{0,31},{1,0},{2,1},{3,2},{4,3},{5,4},{6,5},{7,6},{8,7},{9,8},{10,9... | collective-permute-start | bytes 36872 | tf_op jit(solution)/shard_map/ppermute | solution.py:442
  97.1 6.2 %collective-permute-start.26 = (f32[8,384]{1,0:T(8,128)S(1)}, f32[8,384]{1,0:T(8,128)S(1)}, u32[]{:S(2)}, u32[]{:S(2)}) collective-permute-start(f32[8,384]{1,0:T(8,128)S(1)} %get-tuple-element.161), channel_id=1, source_target_pairs={{0,1},{1,2},{2,3},{3,4},{4,5},{5,6},{6,7},{7,8},{8,9},{9,10},{10,1... | collective-permute-start | bytes 36872 | tf_op jit(solution)/shard_map/ppermute | solution.py:442
  103.7 2.5 %collective-permute-start.28 = (f32[8,384]{1,0:T(8,128)S(1)}, f32[8,384]{1,0:T(8,128)S(1)}, u32[]{:S(2)}, u32[]{:S(2)}) collective-permute-start(f32[8,384]{1,0:T(8,128)S(1)} %get-tuple-element.140), channel_id=1, source_target_pairs={{0,32},{32,64},{64,96},{96,128},{128,160},{160,192},{192,224},{224... | collective-permute-start | bytes 36872 | tf_op jit(solution)/shard_map/ppermute | solution.py:442
  104.9 4.3 %collective-permute-start.29 = (f32[8,384]{1,0:T(8,128)S(1)}, f32[8,384]{1,0:T(8,128)S(1)}, u32[]{:S(2)}, u32[]{:S(2)}) collective-permute-start(f32[8,384]{1,0:T(8,128)S(1)} %get-tuple-element.141), channel_id=1, source_target_pairs={{0,224},{32,0},{64,32},{96,64},{128,96},{160,128},{192,160},{224,1... | collective-permute-start | bytes 36872 | tf_op jit(solution)/shard_map/ppermute | solution.py:442
  109.3 2.9 %collective-permute-start.31 = (f32[8,384]{1,0:T(8,128)S(1)}, f32[8,384]{1,0:T(8,128)S(1)}, u32[]{:S(2)}, u32[]{:S(2)}) collective-permute-start(f32[8,384]{1,0:T(8,128)S(1)} %get-tuple-element.158), channel_id=1, source_target_pairs={{0,31},{1,0},{2,1},{3,2},{4,3},{5,4},{6,5},{7,6},{8,7},{9,8},{10,9... | collective-permute-start | bytes 36872 | tf_op jit(solution)/shard_map/ppermute | solution.py:442
  109.3 5.9 %collective-permute-start.30 = (f32[8,384]{1,0:T(8,128)S(1)}, f32[8,384]{1,0:T(8,128)S(1)}, u32[]{:S(2)}, u32[]{:S(2)}) collective-permute-start(f32[8,384]{1,0:T(8,128)S(1)} %get-tuple-element.159), channel_id=1, source_target_pairs={{0,1},{1,2},{2,3},{3,4},{4,5},{5,6},{6,7},{7,8},{8,9},{9,10},{10,1... | collective-permute-start | bytes 36872 | tf_op jit(solution)/shard_map/ppermute | solution.py:442
  116.4 2.1 %collective-permute-start.32 = (f32[8,384]{1,0:T(8,128)S(1)}, f32[8,384]{1,0:T(8,128)S(1)}, u32[]{:S(2)}, u32[]{:S(2)}) collective-permute-start(f32[8,384]{1,0:T(8,128)S(1)} %get-tuple-element.147), channel_id=1, source_target_pairs={{0,32},{32,64},{64,96},{96,128},{128,160},{160,192},{192,224},{224... | collective-permute-start | bytes 36872 | tf_op jit(solution)/shard_map/ppermute | solution.py:442
  117.7 4.3 %collective-permute-start.33 = (f32[8,384]{1,0:T(8,128)S(1)}, f32[8,384]{1,0:T(8,128)S(1)}, u32[]{:S(2)}, u32[]{:S(2)}) collective-permute-start(f32[8,384]{1,0:T(8,128)S(1)} %get-tuple-element.148), channel_id=1, source_target_pairs={{0,224},{32,0},{64,32},{96,64},{128,96},{160,128},{192,160},{224,1... | collective-permute-start | bytes 36872 | tf_op jit(solution)/shard_map/ppermute | solution.py:442
  122.0 2.9 %collective-permute-start.35 = (f32[8,384]{1,0:T(8,128)S(1)}, f32[8,384]{1,0:T(8,128)S(1)}, u32[]{:S(2)}, u32[]{:S(2)}) collective-permute-start(f32[8,384]{1,0:T(8,128)S(1)} %get-tuple-element.156), channel_id=1, source_target_pairs={{0,31},{1,0},{2,1},{3,2},{4,3},{5,4},{6,5},{7,6},{8,7},{9,8},{10,9... | collective-permute-start | bytes 36872 | tf_op jit(solution)/shard_map/ppermute | solution.py:442
  122.0 5.9 %collective-permute-start.34 = (f32[8,384]{1,0:T(8,128)S(1)}, f32[8,384]{1,0:T(8,128)S(1)}, u32[]{:S(2)}, u32[]{:S(2)}) collective-permute-start(f32[8,384]{1,0:T(8,128)S(1)} %get-tuple-element.157), channel_id=1, source_target_pairs={{0,1},{1,2},{2,3},{3,4},{4,5},{5,6},{6,7},{7,8},{8,9},{9,10},{10,1... | collective-permute-start | bytes 36872 | tf_op jit(solution)/shard_map/ppermute | solution.py:442
